TPU v7x, 32 devices: a whole 2x2x4 slice. The times are simulated.
32 devices in a mesh: pairs: 2 (over x), rows: 8 (over z, y), cols: 2 (over core).
Axes of the slice: x: 2, y: 2, z: 4, core: 2. Of those that a mesh axis runs over, the one named last changes fastest.
Arguments:
- left_feat: bfloat16 [32, 512, 256], P(('pairs', 'rows'), 'cols'), parts along dimension 0, may hold values from -6 to 6
- right_feat: bfloat16 [32, 512, 256], P(('pairs', 'rows'), 'cols'), parts along dimension 0, may hold values from -6 to 6
- block_list: int32 [16, 8, 2], P(('pairs', 'rows'), 'cols'), parts along dimension 0, may hold values from 0 to 1, as said below
- block_count: int32 [16, 8], P(('pairs', 'rows'), 'cols'), parts along dimension 0, may hold values from 1 to 2
- spatial_first: bfloat16 [3, 3, 16, 16], replicated, may hold values from -0.75 to 0.75
- spatial_second: bfloat16 [3, 3, 16, 16], replicated, may hold values from -0.75 to 0.75
- disparity_weight: bfloat16 [17, 16], replicated, may hold values from -0.5 to 0.5
Outputs:
- cost: float32 [32, 512, 256], P(('pairs', 'rows'), 'cols'), parts along dimension 0
There are 2 independent parts, one for each index of `pairs`. A program takes and returns all parts, laid end to end along the dimension named above; an argument that names none is the same for every part. Nothing has to cross between parts.
Inputs may be any that keep to these rules, and one draw needn't show every extreme that they name: `block_list`: for each tile the 2 entries are different block numbers; entries in slots at or past the tile's block_count are not listed.
All inputs are finite; a program needn't handle non-finite values.
Results may differ from a plain program's by a relative error of at most 0.0059.
Values may be sent and summed in bfloat16 or wider, within the bound.
No kernel may reach another device: no remote copies, remote signals or barrier semaphores. Data moves between devices by JAX's collectives and lax.ppermute only.
A program may use at most 128 MiB of HBM per device.

v0:
```python
import functools

import jax
import jax.numpy as jnp
import numpy as np
from jax import lax
from jax.experimental import pallas as pl
from jax.experimental.pallas import tpu as pltpu
from jax.sharding import PartitionSpec as P

G = 16
DB = 128
NBLK = 2
TILE = 64
TAPS = 17
BF = jnp.bfloat16
F32 = jnp.float32
NT = (((1,), (1,)), ((), ()))


def shifted(x, axis, by):
    count = lax.axis_size(axis)
    pairs = [(i, i + by) for i in range(count) if 0 <= i + by < count]
    return lax.ppermute(x, axis, pairs)


def toeplitz(weights, out_cols, out_rows, order):
    in_cols, in_rows = out_cols + 2, out_rows + 2
    pick = np.zeros((out_cols, out_rows, in_cols, in_rows, 3, 3), np.float32)
    for xo in range(out_cols):
        for yo in range(out_rows):
            for i in range(3):
                for j in range(3):
                    pick[xo, yo, xo + j, yo + i, i, j] = 1.0
    pick = pick.reshape(-1, 9).astype(BF)
    flat = weights.reshape(9, G * G)
    full = jnp.dot(pick, flat, preferred_element_type=F32).astype(BF)
    full = full.reshape(out_cols, out_rows, in_cols, in_rows, G, G)
    full = full.transpose(order + (2, 3, 5))
    return full.reshape(out_cols * out_rows * G, in_cols * in_rows * G)


def banded(weights, ndisp):
    e = lax.broadcasted_iota(jnp.int32, (G, ndisp, ndisp), 1)
    d = lax.broadcasted_iota(jnp.int32, (G, ndisp, ndisp), 2)
    tap = ndisp - 1 - e - d + TAPS // 2
    out = jnp.zeros((G, ndisp, ndisp), BF)
    for k in range(TAPS):
        out = jnp.where(tap == k, weights[k][:, None, None], out)
    return out.reshape(G * ndisp, ndisp)


def kernel(
    edge_ref, up, own, dn, up_n, own_n, dn_n, w1, w2, tm, out_ref,
    corr, hidden, second, left_zero, masks,
    *, cols, ndisp,
):
    channels = own.shape[1]
    is_left = edge_ref[2] == 1
    is_right = edge_ref[3] == 1
    group_of = lax.broadcasted_iota(jnp.int32, (G, channels), 1) // (channels // G)
    gmask = jnp.where(
        group_of == lax.broadcasted_iota(jnp.int32, (G, channels), 0), (channels // G) ** -0.5, 0.0
    ).astype(F32)
    lane = lax.broadcasted_iota(jnp.int32, (G, ndisp), 1)
    rows = 6

    def put(xx, y, value):
        start = pl.multiple_of((xx * rows + y) * G, G)
        corr[pl.ds(start, G), :] = value

    def spread(lines):
        lines = lines.astype(F32)
        return jnp.concatenate(
            [(lines[i : i + 1, :] * gmask).astype(BF) for i in range(lines.shape[0])], axis=0
        )

    for band, (b, n) in enumerate(((up, up_n), (own, own_n), (dn, dn_n))):
        masks[...] = b[4 * cols : 4 * cols + 16, :].astype(F32)
        mask_n = n[4 * cols : 4 * cols + 16, :].astype(F32)
        for yb in range(2):
            y = 2 * band + yb
            r_own = (2 + yb) * cols
            left_zero[...] = jnp.where(is_left, jnp.zeros((), BF), n[r_own : r_own + cols, :])

            def block(k, carry, b=b, yb=yb, y=y, r_own=r_own):
                x0 = k * 16
                lines = b[pl.ds(pl.multiple_of(yb * cols + x0, 16), 16), :]
                a = spread(lines)
                hi = lax.dot_general(a, b[r_own : r_own + cols, :], NT, preferred_element_type=F32)
                lo = lax.dot_general(a, left_zero[...], NT, preferred_element_type=F32)
                m = masks[pl.ds(k, 1), :]
                for i in range(16):
                    x = x0 + i
                    s = jnp.where(lane <= x, hi[i * G : i * G + G], lo[i * G : i * G + G])
                    s = pltpu.roll(s, ndisp - 1 - x, 1)
                    put(x + 2, y, (s * m).astype(BF))
                return carry

            lax.fori_loop(0, cols // 16, block, 0)

            tail = n[yb * cols + cols - 16 : yb * cols + cols, :][14:16]
            head = n[yb * cols : yb * cols + 16, :][0:2]
            a = spread(jnp.concatenate([tail, head], axis=0))
            p_n = lax.dot_general(a, n[r_own : r_own + cols, :], NT, preferred_element_type=F32)
            p_o = lax.dot_general(a, b[r_own : r_own + cols, :], NT, preferred_element_type=F32)
            m_l = jnp.where(is_left, 0.0, mask_n[15:16])
            m_r = jnp.where(is_right, 0.0, mask_n[0:1])
            s = jnp.where(lane <= ndisp - 2, p_n[0:G], 0.0)
            put(0, y, (pltpu.roll(s, 1, 1) * m_l).astype(BF))
            put(1, y, (p_n[G : 2 * G] * m_l).astype(BF))
            s = jnp.where(lane <= 0, p_n[2 * G : 3 * G], p_o[2 * G : 3 * G])
            put(cols + 2, y, (pltpu.roll(s, ndisp - 1, 1) * m_r).astype(BF))
            s = jnp.where(lane <= 1, p_n[3 * G : 4 * G], p_o[3 * G : 4 * G])
            put(cols + 3, y, (pltpu.roll(s, ndisp - 2, 1) * m_r).astype(BF))

    step1 = 3
    k1 = (step1 + 2) * rows * G
    m1 = step1 * 4 * G

    def first(s, carry):
        data = corr[pl.ds(pl.multiple_of(s * (step1 * rows * G), 16), k1), :]
        h = jnp.dot(w1[...], data, preferred_element_type=F32)
        hidden[pl.ds(pl.multiple_of(s * m1, 16), m1), :] = jnp.maximum(h, 0.0).astype(BF)
        return carry

    lax.fori_loop(0, (cols + 2) // step1, first, 0)

    zero = jnp.zeros((G, ndisp), BF)
    for which, row in ((0, 0), (1, 3)):
        @pl.when(edge_ref[which] == 1)
        def _():
            def clear(i, carry):
                hidden[pl.ds(pl.multiple_of((i * 4 + row) * G, G), G), :] = zero
                return carry

            lax.fori_loop(0, cols + 2, clear, 0)

    for which, col in ((2, 0), (3, cols + 1)):
        @pl.when(edge_ref[which] == 1)
        def _():
            hidden[col * 4 * G : (col + 1) * 4 * G, :] = jnp.zeros((4 * G, ndisp), BF)

    def next_hidden(u, carry):
        halves = []
        for v in range(2):
            start = pl.multiple_of((2 * u + v) * (8 * 4 * G), 16)
            data = hidden[pl.ds(start, 10 * 4 * G), :]
            h = jnp.dot(w2[...], data, preferred_element_type=F32)
            halves.append(jnp.maximum(h, 0.0))
        for y in range(2):
            for o in range(G):
                r = (y * G + o) * 8
                both = jnp.concatenate([halves[0][r : r + 8], halves[1][r : r + 8]], axis=0)
                second[y, pl.ds(pl.multiple_of(u * 16, 16), 16), o * ndisp : (o + 1) * ndisp] = (
                    both.astype(BF)
                )
        return carry

    lax.fori_loop(0, cols // 16, next_hidden, 0)

    for y in range(2):
        out_ref[y] = jnp.dot(second[y], tm[...], preferred_element_type=F32)


def tile_masks(block_list, block_count, cols, ndisp):
    slot_ids = jnp.arange(block_list.shape[2], dtype=jnp.int32)
    live = slot_ids[None, :] < block_count[0][:, None]
    block_ids = jnp.arange(NBLK, dtype=jnp.int32)
    hits = (block_list[0][..., None] == block_ids) & live[..., None]
    active = jnp.any(hits, axis=1)
    lane_block = (ndisp - 1 - jnp.arange(ndisp)) // DB
    lanes = jnp.where(lane_block[None, :] == 0, active[:, :1], active[:, 1:2])
    return jnp.repeat(lanes.astype(BF), TILE // 16, axis=0)


def body(
    left_feat, right_feat, block_list, block_count, spatial_first, spatial_second, disparity_weight
):
    row_count, cols, channels = left_feat.shape
    ndisp = NBLK * DB
    masks = tile_masks(block_list, block_count, cols, ndisp)
    pack = jnp.concatenate(
        [left_feat.reshape(-1, channels), right_feat.reshape(-1, channels), masks], axis=0
    )
    up = shifted(pack, "rows", 1)
    dn = shifted(pack, "rows", -1)
    swap = [(0, 1), (1, 0)]
    own_n = lax.ppermute(pack, "cols", swap)
    up_n = lax.ppermute(up, "cols", swap)
    dn_n = lax.ppermute(dn, "cols", swap)
    row = lax.axis_index("rows")
    col = lax.axis_index("cols")
    edges = jnp.stack(
        [row == 0, row == lax.axis_size("rows") - 1, col == 0, col == lax.axis_size("cols") - 1]
    ).astype(jnp.int32)
    w1 = toeplitz(spatial_first, 3, 4, (0, 1, 4))
    w2 = toeplitz(spatial_second, 8, 2, (1, 4, 0))
    tm = banded(disparity_weight, ndisp)
    vmem = pl.BlockSpec(memory_space=pltpu.VMEM)
    return pl.pallas_call(
        functools.partial(kernel, cols=cols, ndisp=ndisp),
        out_shape=jax.ShapeDtypeStruct((row_count, cols, ndisp), F32),
        in_specs=[pl.BlockSpec(memory_space=pltpu.SMEM)] + [vmem] * 9,
        out_specs=vmem,
        scratch_shapes=[
            pltpu.VMEM(((cols + 4) * 6 * G, ndisp), BF),
            pltpu.VMEM(((cols + 2) * 4 * G, ndisp), BF),
            pltpu.VMEM((2, cols, G * ndisp), BF),
            pltpu.VMEM((cols, channels), BF),
            pltpu.VMEM((16, ndisp), F32),
        ],
        compiler_params=pltpu.CompilerParams(vmem_limit_bytes=56 * 1024 * 1024),
    )(edges, up, pack, dn, up_n, own_n, dn_n, w1, w2, tm)


def solution(mesh):
    in_specs = (
        P(("pairs", "rows"), "cols", None),
        P(("pairs", "rows"), "cols", None),
        P(("pairs", "rows"), "cols", None),
        P(("pairs", "rows"), "cols"),
        P(),
        P(),
        P(),
    )
    out_specs = P(("pairs", "rows"), "cols", None)
    return jax.shard_map(body, mesh=mesh, in_specs=in_specs, out_specs=out_specs, check_vma=False)
```

profile of v0, /device:TPU:0, one launch (start us, length us, event | category | flops | bytes accessed | tf_op | source)
XLA Modules:
  0.0 110.1 jit_solution(9663423629582446588)
XLA Ops:
  0.0 0.0 copy-start.2
  0.0 0.0 copy-start.3
  0.0 0.7 iota_compare_fusion.1
  0.7 0.8 fusion.35
  1.5 0.2 slice_reduce_fusion.18
  1.7 0.1 select_convert_fusion
  1.8 1.1 pad_maximum_fusion.own
  2.8 0.0 copy-start
  2.8 5.7 %collective-permute-start = (bf16[1040,256]{1,0:T(8,128)(2,1)S(1)}, bf16[1040,256]{1,0:T(8,128)(2,1)}, u32[]{:S(2)}, u32[]{:S(2)}) collective-permute-start(bf16[1040,256]{1,0:T(8,128)(2,1)S(1)} %pad_maximum_fusion.own), channel_id=1, source_target_pairs={{0,2},{2,4},{4,6},{6,8},{8,10},{10,12},{12,14},{1,3},{3,5},{5,7},{... | collective-permute-start | bytes 1597448 | tf_op jit(solution)/shard_map/ppermute | solution.py:24
  8.5 1.3 %collective-permute-start.1 = (bf16[1040,256]{1,0:T(8,128)(2,1)S(1)}, bf16[1040,256]{1,0:T(8,128)(2,1)}, u32[]{:S(2)}, u32[]{:S(2)}) collective-permute-start(bf16[1040,256]{1,0:T(8,128)(2,1)S(1)} %pad_maximum_fusion.own), channel_id=1, source_target_pairs={{2,0},{4,2},{6,4},{8,6},{10,8},{12,10},{14,12},{3,1},{5,3},{7,5},{... | collective-permute-start | bytes 1597448 | tf_op jit(solution)/shard_map/ppermute | solution.py:24
  9.8 0.1 collective-permute-start.3
  10.0 1.8 %slice_reduce_fusion.16 = (bf16[16]{0:T(256)(128)(2,1)S(1)}, bf16[16]{0:T(256)(128)(2,1)S(1)}, bf16[16]{0:T(256)(128)(2,1)S(1)}, bf16[16]{0:T(256)(128)(2,1)S(1)...) fusion(bf16[17,16]{0,1:T(8,128)(2,1)} %param.15), kind=kLoop, calls=%fused_computation.73 | loop fusion | bytes 1088 | tf_op jit(solution)/shard_map/slice | solution.py:49
  11.7 0.1 broadcast_bitcast_fusion.1
  11.9 0.1 broadcast_bitcast_fusion.3
  12.0 0.1 broadcast_bitcast_fusion.5
  12.1 0.1 broadcast_bitcast_fusion.7
  12.2 0.1 broadcast_bitcast_fusion.9
  12.3 0.1 broadcast_bitcast_fusion.11
  12.4 0.1 broadcast_bitcast_fusion.13
  12.5 0.1 broadcast_bitcast_fusion.15
  12.6 0.1 broadcast_bitcast_fusion.17
  12.7 11.9 %fusion.17.tm = bf16[4096,256]{1,0:T(8,128)(2,1)} fusion(s32[4096]{0:T(1024)S(1)} %bitcast.80, bf16[4096]{0:T(1024)(128)(2,1)S(1)} %bitcast.81, bf16[4096]{0:T(1024)(128)(2,1)S(1)} %bitcast.82, bf16[4096]{0:T(1024)(128)(2,1)S(1)} %bitcast.83, bf16[4096]{0:T(1024)(128)(2,1)S(1)} %bitcast.84, bf16[4096]{0:T(1024)(128)(2,1)S(1)} %bitcast.85, ...), kind=kLoop, calls=%fused_computation.18 | loop fusion | flops 37748736 | bytes 2252800 | tf_op jit(solution)/shard_map/jit(_where)/select_n | solution.py:49
  24.6 0.0 copy-done.3
  24.6 0.1 reshape.113
  24.7 5.8 %collective-permute-done.up = bf16[1040,256]{1,0:T(8,128)(2,1)} collective-permute-done((bf16[1040,256]{1,0:T(8,128)(2,1)S(1)}, bf16[1040,256]{1,0:T(8,128)(2,1)}, u32[]{:S(2)}, u32[]{:S(2)}) %collective-permute-start) | collective-permute-done | bytes 532512 | tf_op jit(solution)/shard_map/ppermute | solution.py:24
  30.5 0.0 collective-permute-start.2
  30.5 0.0 collective-permute-done.1.dn
  30.5 0.5 collective-permute-start.4
  31.0 0.0 copy-done.2
  31.0 0.2 convolution_convert_fusion.1
  31.2 1.0 reshape.114
  32.2 0.0 copy-done
  32.2 0.0 copy-start.4
  32.2 1.0 copy.17
  33.2 0.0 copy-start.1
  33.2 0.9 reshape.115
  34.1 0.9 copy.19.w1
  34.9 0.0 copy-done.4
  34.9 0.1 reshape.116
  35.1 0.0 copy-done.1
  35.1 0.2 convolution_convert_fusion
  35.3 1.8 %reshape.117 = bf16[8,2,10,4,16,16]{5,4,3,2,1,0:T(8,128)(2,1)S(1)} reshape(bf16[640,256]{1,0:T(8,128)(2,1)S(1)} %convolution_convert_fusion) | data formatting | bytes 655360 | tf_op jit(solution)/shard_map/reshape | solution.py:38
  37.0 2.9 %copy.39 = bf16[8,2,10,4,16,16]{5,3,2,0,4,1:T(4,128)(2,1)} copy(bf16[8,2,10,4,16,16]{5,4,3,2,1,0:T(8,128)(2,1)S(1)} %reshape.117) | data formatting | bytes 655360 | tf_op jit(solution)/shard_map/reshape | solution.py:38
  40.0 5.0 %reshape.118.w2 = bf16[256,640]{1,0:T(8,128)(2,1)} reshape(bf16[2,16,8,10,4,16]{5,4,3,2,1,0:T(4,128)(2,1)} %bitcast.76) | data formatting | bytes 655360 | tf_op jit(solution)/shard_map/reshape | solution.py:40
  44.9 0.7 add_convert_fusion.edge_ref
  45.6 0.0 collective-permute-done.3.own_n
  45.6 0.0 collective-permute-done.2.up_n
  45.6 0.0 collective-permute-done.4.dn_n
  45.6 64.5 %shard_map.91 = f32[2,256,256]{2,1,0:T(8,128)} custom-call(s32[4]{0:T(128)} %add_convert_fusion.edge_ref, bf16[1040,256]{1,0:T(8,128)(2,1)} %collective-permute-done.up, bf16[1040,256]{1,0:T(8,128)(2,1)} %copy-done, bf16[1040,256]{1,0:T(8,128)(2,1)} %collective-permute-done.1.dn, bf16[1040,256]{1,0:T(8,128)(2,1)} %collective-permute-done.2.up_n, ...), custom_call_target="tpu_custom_call" | custom-call | tf_op jit(solution)/shard_map/pallas_call | solution.py:201
  (23 shorter events, 0.2 us)
Async XLA Ops:
  0.0 31.0 %copy-start.2 = (bf16[360,9]{1,0:T(8,128)(2,1)S(1)}, bf16[360,9]{1,0:T(8,128)(2,1)}, u32[]{:S(2)}) copy-start(bf16[360,9]{1,0:T(8,128)(2,1)} %constant.70.clone) | copy-start | bytes 19444
  0.0 24.6 %copy-start.3 = (bf16[3,3,16,16]{3,2,1,0:T(8,128)(2,1)S(1)}, bf16[3,3,16,16]{3,2,1,0:T(8,128)(2,1)}, u32[]{:S(2)}) copy-start(bf16[3,3,16,16]{3,2,1,0:T(8,128)(2,1)} %param.13) | copy-start | bytes 13828
  2.8 29.3 %copy-start = (bf16[1040,256]{1,0:T(8,128)(2,1)}, bf16[1040,256]{1,0:T(8,128)(2,1)S(1)}, u32[]{:S(2)}) copy-start(bf16[1040,256]{1,0:T(8,128)(2,1)S(1)} %pad_maximum_fusion.own) | copy-start | bytes 1597444
  2.8 27.6 %collective-permute-start = (bf16[1040,256]{1,0:T(8,128)(2,1)S(1)}, bf16[1040,256]{1,0:T(8,128)(2,1)}, u32[]{:S(2)}, u32[]{:S(2)}) collective-permute-start(bf16[1040,256]{1,0:T(8,128)(2,1)S(1)} %pad_maximum_fusion.own), channel_id=1, source_target_pairs={{0,2},{2,4},{4,6},{6,8},{8,10},{10,12},{12,14},{1,3},{3,5},{5,7},{... | collective-permute-start | bytes 1597448 | tf_op jit(solution)/shard_map/ppermute | solution.py:24
  8.5 21.9 %collective-permute-start.1 = (bf16[1040,256]{1,0:T(8,128)(2,1)S(1)}, bf16[1040,256]{1,0:T(8,128)(2,1)}, u32[]{:S(2)}, u32[]{:S(2)}) collective-permute-start(bf16[1040,256]{1,0:T(8,128)(2,1)S(1)} %pad_maximum_fusion.own), channel_id=1, source_target_pairs={{2,0},{4,2},{6,4},{8,6},{10,8},{12,10},{14,12},{3,1},{5,3},{7,5},{... | collective-permute-start | bytes 1597448 | tf_op jit(solution)/shard_map/ppermute | solution.py:24
  9.8 35.8 %collective-permute-start.3 = (bf16[1040,256]{1,0:T(8,128)(2,1)S(1)}, bf16[1040,256]{1,0:T(8,128)(2,1)}, u32[]{:S(2)}, u32[]{:S(2)}) collective-permute-start(bf16[1040,256]{1,0:T(8,128)(2,1)S(1)} %pad_maximum_fusion.own), channel_id=1, source_target_pairs={{0,1},{1,0},{2,3},{3,2},{4,5},{5,4},{6,7},{7,6},{8,9},{9,8},{10,11... | collective-permute-start | bytes 1597448 | tf_op jit(solution)/shard_map/ppermute | solution.py:189
  30.5 15.1 %collective-permute-start.2 = (bf16[1040,256]{1,0:T(8,128)(2,1)}, bf16[1040,256]{1,0:T(8,128)(2,1)}, u32[]{:S(2)}, u32[]{:S(2)}) collective-permute-start(bf16[1040,256]{1,0:T(8,128)(2,1)} %collective-permute-done.up), channel_id=1, source_target_pairs={{0,1},{1,0},{2,3},{3,2},{4,5},{5,4},{6,7},{7,6},{8,9},{9,8},{10,11... | collective-permute-start | bytes 1597448 | tf_op jit(solution)/shard_map/ppermute | solution.py:190
  30.5 15.1 %collective-permute-start.4 = (bf16[1040,256]{1,0:T(8,128)(2,1)}, bf16[1040,256]{1,0:T(8,128)(2,1)}, u32[]{:S(2)}, u32[]{:S(2)}) collective-permute-start(bf16[1040,256]{1,0:T(8,128)(2,1)} %collective-permute-done.1.dn), channel_id=1, source_target_pairs={{0,1},{1,0},{2,3},{3,2},{4,5},{5,4},{6,7},{7,6},{8,9},{9,8},{10,11... | collective-permute-start | bytes 1597448 | tf_op jit(solution)/shard_map/ppermute | solution.py:191
  32.2 2.8 %copy-start.4 = (bf16[3,3,16,16]{3,2,1,0:T(8,128)(2,1)S(1)}, bf16[3,3,16,16]{3,2,1,0:T(8,128)(2,1)}, u32[]{:S(2)}) copy-start(bf16[3,3,16,16]{3,2,1,0:T(8,128)(2,1)} %param.14) | copy-start | bytes 13828
  33.2 1.9 %copy-start.1 = (bf16[640,9]{1,0:T(8,128)(2,1)S(1)}, bf16[640,9]{1,0:T(8,128)(2,1)}, u32[]{:S(2)}) copy-start(bf16[640,9]{1,0:T(8,128)(2,1)} %constant.71.clone) | copy-start | bytes 34564
where the time goes:
time: 110 us
  Pallas kernels  64.5 us (59%)
  local copies, waits for them, and re-layouts  16.4 us (15%)
  other arithmetic  15.2 us (14%)
  starting transfers between devices  7.56 us (7%)
  waiting for transfers between devices  5.77 us (5%)
    pallas_call x1, Pallas kernels, body(): pl.pallas_call(functools.partial(kernel, cols=cols, ndisp=ndisp), out_sha...  64.5 us
    select_n x1, other arithmetic, banded(): out = jnp.where(tap == k, weights[k][:, None, None], out)  11.9 us
    ppermute x2, starting transfers between devices, shifted(): return lax.ppermute(x, axis, pairs)  6.98 us
    reshape x3, local copies, waits for them, and re-layouts, toeplitz(): return full.reshape(out_cols * out_rows * G, in_cols * in_rows * G)  6.75 us
    reshape x4, local copies, waits for them, and re-layouts, toeplitz(): full = full.reshape(out_cols, out_rows, in_cols, in_rows, G, G)  6.62 us
    ppermute x2, waiting for transfers between devices, shifted(): return lax.ppermute(x, axis, pairs)  5.76 us
  transfers between devices with their start and end apart: 5, of which 1 were waited for; matrix products, arithmetic and copies ran while one was open for 27% of the time, Pallas kernels for 0%

commit v1 on v0

v1 whole, which is shorter than its diff:
```python
import functools

import jax
import jax.numpy as jnp
from jax import lax
from jax.experimental import pallas as pl
from jax.experimental.pallas import tpu as pltpu
from jax.sharding import PartitionSpec as P

G = 16
DB = 128
NBLK = 2
TILE = 64
TAPS = 17
BF = jnp.bfloat16
F32 = jnp.float32
NT = (((1,), (1,)), ((), ()))


def shifted(x, axis, by):
    count = lax.axis_size(axis)
    pairs = [(i, i + by) for i in range(count) if 0 <= i + by < count]
    return lax.ppermute(x, axis, pairs)


def tap_row(weights, in_rows, width):
    taps = weights.transpose(2, 1, 0, 3)
    taps = jnp.pad(taps, ((0, 0), (0, 0), (0, in_rows - 3), (0, 0)))
    taps = taps.reshape(G, 3 * in_rows * G)
    return jnp.pad(taps, ((0, 0), (0, width - taps.shape[1]))).astype(F32)


def banded(weights, ndisp):
    e = lax.broadcasted_iota(jnp.int32, (G, ndisp, ndisp), 1)
    d = lax.broadcasted_iota(jnp.int32, (G, ndisp, ndisp), 2)
    tap = ndisp - 1 - e - d + TAPS // 2
    out = jnp.zeros((G, ndisp, ndisp), BF)
    for k in range(TAPS):
        out = jnp.where(tap == k, weights[k][:, None, None], out)
    return out.reshape(G * ndisp, ndisp)


def kernel(
    edge_ref, up, own, dn, up_n, own_n, dn_n, t1, t2, tm, out_ref,
    xs, xn, corr, hidden, second, left_zero, w1, w2, sems,
    *, cols, ndisp,
):
    channels = xs.shape[2]
    rows = 6
    is_left = edge_ref[2] == 1
    is_right = edge_ref[3] == 1
    copies = []
    for i, (src, dst) in enumerate(
        ((own, xs.at[1]), (own_n, xn.at[1]), (up, xs.at[0]), (up_n, xn.at[0]), (dn, xs.at[2]), (dn_n, xn.at[2]))
    ):
        copies.append(pltpu.make_async_copy(src, dst, sems.at[i]))
        copies[-1].start()

    wide1, wide2 = t1.shape[1], t2.shape[1]
    for xo in range(3):
        for yo in range(4):
            r = (xo * 4 + yo) * G
            moved = pltpu.roll(t1[...], (xo * 6 + yo) * G, 1)
            w1[r : r + G, :] = moved.astype(BF)[:, : w1.shape[1]]
    blocks = []
    for yo in range(2):
        for xo in range(8):
            by = (xo * 4 + yo) * G
            blocks.append((pltpu.roll(t2[...], by, 1) if by else t2[...]).astype(BF))
    plain = jnp.concatenate(blocks, axis=0)
    r = lax.broadcasted_iota(jnp.int32, (256, 256), 0)
    c = lax.broadcasted_iota(jnp.int32, (256, 256), 1)
    order = (r // 128) * 128 + (r % 8) * G + (r // 8) % G
    order = jnp.where(c == order, 1.0, 0.0).astype(BF)
    w2[...] = jnp.dot(order, plain, preferred_element_type=F32).astype(BF)

    for copy in copies:
        copy.wait()

    group_of = lax.broadcasted_iota(jnp.int32, (G, channels), 1) // (channels // G)
    gmask = jnp.where(
        group_of == lax.broadcasted_iota(jnp.int32, (G, channels), 0), (channels // G) ** -0.5, 0.0
    ).astype(F32)
    lane = lax.broadcasted_iota(jnp.int32, (G, ndisp), 1)

    def spread(lines):
        lines = lines.astype(F32)
        return jnp.concatenate(
            [(lines[i : i + 1, :] * gmask).astype(BF) for i in range(lines.shape[0])], axis=0
        )

    def corr_row(y, carry):
        band, yb = y // 2, y % 2

        def put(xx, value):
            corr[pl.ds(pl.multiple_of((xx * rows + y) * G, G), G), :] = value.astype(BF)

        def pixels(ref, x0, count):
            return ref[band, pl.ds(pl.multiple_of(yb * cols + x0, 16), count), :]

        r_start = pl.multiple_of((2 + yb) * cols, 16)
        near = xn[band, pl.ds(r_start, cols), :]
        left_zero[...] = jnp.where(is_left, jnp.zeros_like(near), near)
        masks = xs[band, 4 * cols : 4 * cols + 16, :].astype(F32)
        for k in range(cols // 16):
            x0 = k * 16
            a = spread(pixels(xs, x0, 16))
            hi = lax.dot_general(a, xs[band, pl.ds(r_start, cols), :], NT, preferred_element_type=F32)
            lo = lax.dot_general(a, left_zero[...], NT, preferred_element_type=F32)
            m = masks[k : k + 1]
            for i in range(16):
                x = x0 + i
                s = jnp.where(lane <= x, hi[i * G : i * G + G], lo[i * G : i * G + G])
                if x < ndisp - 1:
                    s = pltpu.roll(s, ndisp - 1 - x, 1)
                put(x + 2, s * m)

        mask_n = xn[band, 4 * cols : 4 * cols + 16, :].astype(F32)
        tail = pixels(xn, cols - 16, 16).astype(F32)[14:16]
        head = pixels(xn, 0, 16).astype(F32)[0:2]
        a = spread(jnp.concatenate([tail, head], axis=0))
        p_n = lax.dot_general(a, xn[band, pl.ds(r_start, cols), :], NT, preferred_element_type=F32)
        p_o = lax.dot_general(a, xs[band, pl.ds(r_start, cols), :], NT, preferred_element_type=F32)
        m_l = jnp.where(is_left, 0.0, mask_n[15:16])
        m_r = jnp.where(is_right, 0.0, mask_n[0:1])
        s = jnp.where(lane <= ndisp - 2, p_n[0:G], 0.0)
        put(0, pltpu.roll(s, 1, 1) * m_l)
        put(1, p_n[G : 2 * G] * m_l)
        s = jnp.where(lane <= 0, p_n[2 * G : 3 * G], p_o[2 * G : 3 * G])
        put(cols + 2, pltpu.roll(s, ndisp - 1, 1) * m_r)
        s = jnp.where(lane <= 1, p_n[3 * G : 4 * G], p_o[3 * G : 4 * G])
        put(cols + 3, pltpu.roll(s, ndisp - 2, 1) * m_r)
        return carry

    lax.fori_loop(0, rows, corr_row, 0)

    step1 = 3
    k1 = (step1 + 2) * rows * G
    m1 = step1 * 4 * G

    def first(s, carry):
        data = corr[pl.ds(pl.multiple_of(s * (step1 * rows * G), 16), k1), :]
        h = jnp.dot(w1[...], data, preferred_element_type=F32)
        hidden[pl.ds(pl.multiple_of(s * m1, 16), m1), :] = jnp.maximum(h, 0.0).astype(BF)
        return carry

    lax.fori_loop(0, -(-(cols + 2) // step1), first, 0, unroll=8)

    zero = jnp.zeros((G, ndisp), BF)
    for which, row in ((0, 0), (1, 3)):
        @pl.when(edge_ref[which] == 1)
        def _():
            def clear(i, carry):
                hidden[pl.ds(pl.multiple_of((i * 4 + row) * G, G), G), :] = zero
                return carry

            lax.fori_loop(0, cols + 2, clear, 0, unroll=8)

    for which, col in ((2, 0), (3, cols + 1)):
        @pl.when(edge_ref[which] == 1)
        def _():
            hidden[col * 4 * G : (col + 1) * 4 * G, :] = jnp.zeros((4 * G, ndisp), BF)

    def next_hidden(u, carry):
        halves = []
        for v in range(2):
            start = pl.multiple_of((2 * u + v) * (8 * 4 * G), 16)
            data = hidden[pl.ds(start, 10 * 4 * G), :]
            h = jnp.dot(w2[...], data, preferred_element_type=F32)
            halves.append(jnp.maximum(h, 0.0))
        for y in range(2):
            for o in range(G):
                r = (y * G + o) * 8
                both = jnp.concatenate([halves[0][r : r + 8], halves[1][r : r + 8]], axis=0)
                second[y, pl.ds(pl.multiple_of(u * 16, 16), 16), o * ndisp : (o + 1) * ndisp] = (
                    both.astype(BF)
                )
        return carry

    lax.fori_loop(0, cols // 16, next_hidden, 0, unroll=4)

    for y in range(2):
        out_ref[y] = jnp.dot(second[y], tm[...], preferred_element_type=F32)


def tile_masks(block_list, block_count, cols, ndisp):
    slot_ids = jnp.arange(block_list.shape[2], dtype=jnp.int32)
    live = slot_ids[None, :] < block_count[0][:, None]
    block_ids = jnp.arange(NBLK, dtype=jnp.int32)
    hits = (block_list[0][..., None] == block_ids) & live[..., None]
    active = jnp.any(hits, axis=1)
    lane_block = (ndisp - 1 - jnp.arange(ndisp)) // DB
    lanes = jnp.where(lane_block[None, :] == 0, active[:, :1], active[:, 1:2])
    return jnp.repeat(lanes.astype(BF), TILE // 16, axis=0)


def body(
    left_feat, right_feat, block_list, block_count, spatial_first, spatial_second, disparity_weight
):
    row_count, cols, channels = left_feat.shape
    ndisp = NBLK * DB
    masks = tile_masks(block_list, block_count, cols, ndisp)
    pack = jnp.concatenate(
        [left_feat.reshape(-1, channels), right_feat.reshape(-1, channels), masks], axis=0
    )
    up = shifted(pack, "rows", 1)
    dn = shifted(pack, "rows", -1)
    swap = [(0, 1), (1, 0)]
    own_n = lax.ppermute(pack, "cols", swap)
    up_n = lax.ppermute(up, "cols", swap)
    dn_n = lax.ppermute(dn, "cols", swap)
    row = lax.axis_index("rows")
    col = lax.axis_index("cols")
    edges = jnp.stack(
        [row == 0, row == lax.axis_size("rows") - 1, col == 0, col == lax.axis_size("cols") - 1]
    ).astype(jnp.int32)
    t1 = tap_row(spatial_first, 6, 512)
    t2 = tap_row(spatial_second, 4, 640)
    tm = banded(disparity_weight, ndisp)
    packed = pack.shape[0]
    steps1 = -(-(cols + 2) // 3)
    vmem = pl.BlockSpec(memory_space=pltpu.VMEM)
    hbm = pl.BlockSpec(memory_space=pl.ANY)
    return pl.pallas_call(
        functools.partial(kernel, cols=cols, ndisp=ndisp),
        out_shape=jax.ShapeDtypeStruct((row_count, cols, ndisp), F32),
        in_specs=[pl.BlockSpec(memory_space=pltpu.SMEM)] + [hbm] * 6 + [vmem] * 3,
        out_specs=vmem,
        scratch_shapes=[
            pltpu.VMEM((3, packed, channels), BF),
            pltpu.VMEM((3, packed, channels), BF),
            pltpu.VMEM(((steps1 * 3 + 2) * 6 * G, ndisp), BF),
            pltpu.VMEM((steps1 * 3 * 4 * G, ndisp), BF),
            pltpu.VMEM((2, cols, G * ndisp), BF),
            pltpu.VMEM((cols, channels), BF),
            pltpu.VMEM((3 * 4 * G, 5 * 6 * G), BF),
            pltpu.VMEM((8 * 2 * G, 10 * 4 * G), BF),
            pltpu.SemaphoreType.DMA((6,)),
        ],
        compiler_params=pltpu.CompilerParams(vmem_limit_bytes=56 * 1024 * 1024),
    )(edges, up, pack, dn, up_n, own_n, dn_n, t1, t2, tm)


def solution(mesh):
    in_specs = (
        P(("pairs", "rows"), "cols", None),
        P(("pairs", "rows"), "cols", None),
        P(("pairs", "rows"), "cols", None),
        P(("pairs", "rows"), "cols"),
        P(),
        P(),
        P(),
    )
    out_specs = P(("pairs", "rows"), "cols", None)
    return jax.shard_map(body, mesh=mesh, in_specs=in_specs, out_specs=out_specs, check_vma=False)
```

time: 110 us -> 73.9 us (0.67)
  Pallas kernels: 64.5 us -> 25.5 us
  waiting for transfers between devices: 5.77 us -> 19.6 us
  local copies, waits for them, and re-layouts: 16.4 us -> 4.87 us
  other arithmetic: 15.2 us -> 16.4 us
    pallas_call x1, Pallas kernels: 64.5 us -> 25.5 us  [body(): pl.pallas_call(functools.partial(kernel, cols=cols, ndisp=ndisp), out_sha...]
    ppermute x2, waiting for transfers between devices: 5.76 us -> 19.6 us  [shifted(): return lax.ppermute(x, axis, pairs)]
    reshape x9 -> x2, local copies, waits for them, and re-layouts: 13.6 us -> 0.21 us  [tap_row(): taps = taps.reshape(G, 3 * in_rows * G)]
    unnamed x38 -> x46, local copies, waits for them, and re-layouts: 0.85 us -> 2.6 us
    convert_element_type x0 -> x2, other arithmetic: none -> 1.22 us  [tap_row(): return jnp.pad(taps, ((0, 0), (0, width - taps.shape[1]))).astype(F32)]
  transfers between devices with their start and end apart: 5 -> 5, of which waited for: 1 -> 2; matrix products, arithmetic and copies ran while one was open for 27% -> 23% of each run, Pallas kernels for 0% -> 0%
where the time goes in v1:
time: 73.9 us; the launch traced here: 73.5 us
  Pallas kernels  25.5 us (35%)
  waiting for transfers between devices  19.6 us (27%)
  other arithmetic  16.4 us (22%)
  starting transfers between devices  6.95 us (9%)
  local copies, waits for them, and re-layouts  4.87 us (7%)
    pallas_call x1, Pallas kernels, body(): pl.pallas_call(functools.partial(kernel, cols=cols, ndisp=ndisp), out_sha...  25.5 us
    ppermute x2, waiting for transfers between devices, shifted(): return lax.ppermute(x, axis, pairs)  19.6 us
    select_n x1, other arithmetic, banded(): out = jnp.where(tap == k, weights[k][:, None, None], out)  11.9 us
    ppermute x2, starting transfers between devices, shifted(): return lax.ppermute(x, axis, pairs)  6.39 us
    unnamed x46, local copies, waits for them, and re-layouts  2.6 us
    slice x1, local copies, waits for them, and re-layouts, banded(): out = jnp.where(tap == k, weights[k][:, None, None], out)  1.79 us
  transfers between devices with their start and end apart: 5, of which 2 were waited for; matrix products, arithmetic and copies ran while one was open for 23% of the time, Pallas kernels for 0%

profile of v1, /device:TPU:0, one launch (start us, length us, event | category | flops | bytes accessed | tf_op | source)
XLA Modules:
  0.0 73.5 jit_solution(11838295597930218868)
XLA Ops:
  0.0 0.0 copy-start.6
  0.0 0.7 iota_compare_fusion.1
  0.7 0.8 %fusion.35 = pred[4,2]{1,0:T(4,128)(4,1)S(1)} fusion(s32[4,2]{0,1:T(2,128)} %bitcast.86, pred[4,2]{0,1:T(4,128)(4,1)S(1)} %iota_compare_fusion.1), kind=kLoop, calls=%fused_computation.75 | loop fusion | flops 40 | bytes 48 | tf_op jit(solution)/shard_map/reduce_or | solution.py:191
  1.4 0.2 slice_reduce_fusion.18
  1.6 0.1 select_convert_fusion
  1.7 0.0 copy-start.7
  1.7 1.1 %pad_maximum_fusion.own = bf16[1040,256]{1,0:T(8,128)(2,1)S(1)} fusion(bf16[16,256]{1,0:T(8,128)(2,1)S(1)} %reshape.100, bf16[512,256]{1,0:T(8,128)(2,1)} %bitcast.64, bf16[512,256]{1,0:T(8,128)(2,1)} %bitcast.65), kind=kLoop, calls=%fused_computation.35 | loop fusion | flops 1597440 | bytes 1064960 | tf_op jit(solution)/shard_map/concatenate | solution.py:203
  2.8 0.0 copy-start
  2.8 0.5 collective-permute-start.3
  3.3 1.3 %collective-permute-start.1 = (bf16[1040,256]{1,0:T(8,128)(2,1)S(1)}, bf16[1040,256]{1,0:T(8,128)(2,1)S(1)}, u32[]{:S(2)}, u32[]{:S(2)}) collective-permute-start(bf16[1040,256]{1,0:T(8,128)(2,1)S(1)} %pad_maximum_fusion.own), channel_id=1, source_target_pairs={{2,0},{4,2},{6,4},{8,6},{10,8},{12,10},{14,12},{3,1},{5,3},{7,5},{... | collective-permute-start | bytes 1597448 | tf_op jit(solution)/shard_map/ppermute | solution.py:23
  4.6 5.1 %collective-permute-start = (bf16[1040,256]{1,0:T(8,128)(2,1)S(1)}, bf16[1040,256]{1,0:T(8,128)(2,1)S(1)}, u32[]{:S(2)}, u32[]{:S(2)}) collective-permute-start(bf16[1040,256]{1,0:T(8,128)(2,1)S(1)} %pad_maximum_fusion.own), channel_id=1, source_target_pairs={{0,2},{2,4},{4,6},{6,8},{8,10},{10,12},{12,14},{1,3},{3,5},{5,7},{... | collective-permute-start | bytes 1597448 | tf_op jit(solution)/shard_map/ppermute | solution.py:23
  9.8 1.8 %slice_reduce_fusion.16 = (bf16[16]{0:T(256)(128)(2,1)S(1)}, bf16[16]{0:T(256)(128)(2,1)S(1)}, bf16[16]{0:T(256)(128)(2,1)S(1)}, bf16[16]{0:T(256)(128)(2,1)S(1)...) fusion(bf16[17,16]{0,1:T(8,128)(2,1)} %param.13), kind=kLoop, calls=%fused_computation.72 | loop fusion | bytes 1088 | tf_op jit(solution)/shard_map/slice | solution.py:39
  11.6 0.1 broadcast_bitcast_fusion.3
  11.6 0.1 broadcast_bitcast_fusion.5
  11.7 0.1 broadcast_bitcast_fusion.7
  11.8 0.1 broadcast_bitcast_fusion.9
  11.9 0.1 broadcast_bitcast_fusion.11
  11.9 0.1 broadcast_bitcast_fusion.13
  12.0 0.1 broadcast_bitcast_fusion.17
  12.3 0.1 broadcast_bitcast_fusion.15
  12.4 0.1 broadcast_bitcast_fusion.1
  12.5 8.0 %collective-permute-done.1.dn = bf16[1040,256]{1,0:T(8,128)(2,1)S(1)} collective-permute-done((bf16[1040,256]{1,0:T(8,128)(2,1)S(1)}, bf16[1040,256]{1,0:T(8,128)(2,1)S(1)}, u32[]{:S(2)}, u32[]{:S(2)}) %collective-permute-start.1) | collective-permute-done | bytes 532512 | tf_op jit(solution)/shard_map/ppermute | solution.py:23
  20.5 0.0 copy-start.2
  20.5 0.0 collective-permute-start.4
  20.5 11.6 %collective-permute-done.up = bf16[1040,256]{1,0:T(8,128)(2,1)S(1)} collective-permute-done((bf16[1040,256]{1,0:T(8,128)(2,1)S(1)}, bf16[1040,256]{1,0:T(8,128)(2,1)S(1)}, u32[]{:S(2)}, u32[]{:S(2)}) %collective-permute-start) | collective-permute-done | bytes 532512 | tf_op jit(solution)/shard_map/ppermute | solution.py:23
  32.1 0.0 copy-start.3
  32.1 0.0 collective-permute-start.2
  32.2 11.9 %fusion.17.tm = bf16[4096,256]{1,0:T(8,128)(2,1)} fusion(s32[4096]{0:T(1024)S(1)} %bitcast.66, bf16[4096]{0:T(1024)(128)(2,1)S(1)} %bitcast.84, bf16[4096]{0:T(1024)(128)(2,1)S(1)} %bitcast.85, bf16[4096]{0:T(1024)(128)(2,1)S(1)} %bitcast.70, bf16[4096]{0:T(1024)(128)(2,1)S(1)} %bitcast.71, bf16[4096]{0:T(1024)(128)(2,1)S(1)} %bitcast.72, ...), kind=kLoop, calls=%fused_computation.18 | loop fusion | flops 37748736 | bytes 2252800 | tf_op jit(solution)/shard_map/jit(_where)/select_n | solution.py:39
  44.0 0.0 copy-done.6
  44.1 0.1 reshape.101
  44.2 0.0 copy-done.7
  44.3 0.1 reshape.102
  44.4 0.7 add_convert_fusion.edge_ref
  45.1 0.6 pad_convert_fusion.1.t1
  45.7 0.6 pad_convert_fusion.t2
  46.3 0.0 collective-permute-done.3.own_n
  46.3 0.0 copy-start.1
  46.3 0.0 collective-permute-done.4.dn_n
  46.3 0.0 copy-start.4
  46.3 0.0 collective-permute-done.2.up_n
  46.3 0.0 copy-done
  46.3 0.0 copy-done.2
  46.3 0.0 copy-done.3
  46.3 0.8 %copy-done.1 = bf16[1040,256]{1,0:T(8,128)(2,1)} copy-done((bf16[1040,256]{1,0:T(8,128)(2,1)}, bf16[1040,256]{1,0:T(8,128)(2,1)S(1)}, u32[]{:S(2)}) %copy-start.1) | copy-done | bytes 532504
  47.1 0.2 copy-done.4
  47.3 0.0 copy-start.5
  47.3 0.8 %copy-done.5 = bf16[1040,256]{1,0:T(8,128)(2,1)} copy-done((bf16[1040,256]{1,0:T(8,128)(2,1)}, bf16[1040,256]{1,0:T(8,128)(2,1)S(1)}, u32[]{:S(2)}) %copy-start.5) | copy-done | bytes 532504
  48.1 25.5 %shard_map.73 = f32[2,256,256]{2,1,0:T(8,128)} custom-call(s32[4]{0:T(128)} %add_convert_fusion.edge_ref, bf16[1040,256]{1,0:T(8,128)(2,1)} %copy-done.3, bf16[1040,256]{1,0:T(8,128)(2,1)} %copy-done, bf16[1040,256]{1,0:T(8,128)(2,1)} %copy-done.2, bf16[1040,256]{1,0:T(8,128)(2,1)} %copy-done.5, bf16[1040,256]{1,0:T(8,128)(2,1)} %copy-done.1, ...), custom_call_target="tpu_custom_call" | custom-call | tf_op jit(solution)/shard_map/pallas_call | solution.py:224
  (27 shorter events, 0.3 us)
Async XLA Ops:
  0.0 44.0 %copy-start.6 = (bf16[3,3,16,16]{3,2,1,0:T(8,128)(2,1)S(1)}, bf16[3,3,16,16]{3,2,1,0:T(8,128)(2,1)}, u32[]{:S(2)}) copy-start(bf16[3,3,16,16]{3,2,1,0:T(8,128)(2,1)} %param.11) | copy-start | bytes 13828
  1.7 42.5 %copy-start.7 = (bf16[3,3,16,16]{3,2,1,0:T(8,128)(2,1)S(1)}, bf16[3,3,16,16]{3,2,1,0:T(8,128)(2,1)}, u32[]{:S(2)}) copy-start(bf16[3,3,16,16]{3,2,1,0:T(8,128)(2,1)} %param.12) | copy-start | bytes 13828
  2.8 43.5 %copy-start = (bf16[1040,256]{1,0:T(8,128)(2,1)}, bf16[1040,256]{1,0:T(8,128)(2,1)S(1)}, u32[]{:S(2)}) copy-start(bf16[1040,256]{1,0:T(8,128)(2,1)S(1)} %pad_maximum_fusion.own) | copy-start | bytes 1597444
  2.8 43.5 %collective-permute-start.3 = (bf16[1040,256]{1,0:T(8,128)(2,1)S(1)}, bf16[1040,256]{1,0:T(8,128)(2,1)S(1)}, u32[]{:S(2)}, u32[]{:S(2)}) collective-permute-start(bf16[1040,256]{1,0:T(8,128)(2,1)S(1)} %pad_maximum_fusion.own), channel_id=1, source_target_pairs={{0,1},{1,0},{2,3},{3,2},{4,5},{5,4},{6,7},{7,6},{8,9},{9,8},{10,11... | collective-permute-start | bytes 1597448 | tf_op jit(solution)/shard_map/ppermute | solution.py:209
  3.3 17.2 %collective-permute-start.1 = (bf16[1040,256]{1,0:T(8,128)(2,1)S(1)}, bf16[1040,256]{1,0:T(8,128)(2,1)S(1)}, u32[]{:S(2)}, u32[]{:S(2)}) collective-permute-start(bf16[1040,256]{1,0:T(8,128)(2,1)S(1)} %pad_maximum_fusion.own), channel_id=1, source_target_pairs={{2,0},{4,2},{6,4},{8,6},{10,8},{12,10},{14,12},{3,1},{5,3},{7,5},{... | collective-permute-start | bytes 1597448 | tf_op jit(solution)/shard_map/ppermute | solution.py:23
  4.6 27.5 %collective-permute-start = (bf16[1040,256]{1,0:T(8,128)(2,1)S(1)}, bf16[1040,256]{1,0:T(8,128)(2,1)S(1)}, u32[]{:S(2)}, u32[]{:S(2)}) collective-permute-start(bf16[1040,256]{1,0:T(8,128)(2,1)S(1)} %pad_maximum_fusion.own), channel_id=1, source_target_pairs={{0,2},{2,4},{4,6},{6,8},{8,10},{10,12},{12,14},{1,3},{3,5},{5,7},{... | collective-permute-start | bytes 1597448 | tf_op jit(solution)/shard_map/ppermute | solution.py:23
  20.5 25.8 %copy-start.2 = (bf16[1040,256]{1,0:T(8,128)(2,1)}, bf16[1040,256]{1,0:T(8,128)(2,1)S(1)}, u32[]{:S(2)}) copy-start(bf16[1040,256]{1,0:T(8,128)(2,1)S(1)} %collective-permute-done.1.dn) | copy-start | bytes 1597444
  20.5 25.8 %collective-permute-start.4 = (bf16[1040,256]{1,0:T(8,128)(2,1)S(1)}, bf16[1040,256]{1,0:T(8,128)(2,1)S(1)}, u32[]{:S(2)}, u32[]{:S(2)}) collective-permute-start(bf16[1040,256]{1,0:T(8,128)(2,1)S(1)} %collective-permute-done.1.dn), channel_id=1, source_target_pairs={{0,1},{1,0},{2,3},{3,2},{4,5},{5,4},{6,7},{7,6},{8,9},{9,8},{10,11... | collective-permute-start | bytes 1597448 | tf_op jit(solution)/shard_map/ppermute | solution.py:211
  32.1 14.2 %copy-start.3 = (bf16[1040,256]{1,0:T(8,128)(2,1)}, bf16[1040,256]{1,0:T(8,128)(2,1)S(1)}, u32[]{:S(2)}) copy-start(bf16[1040,256]{1,0:T(8,128)(2,1)S(1)} %collective-permute-done.up) | copy-start | bytes 1597444
  32.1 14.2 %collective-permute-start.2 = (bf16[1040,256]{1,0:T(8,128)(2,1)S(1)}, bf16[1040,256]{1,0:T(8,128)(2,1)S(1)}, u32[]{:S(2)}, u32[]{:S(2)}) collective-permute-start(bf16[1040,256]{1,0:T(8,128)(2,1)S(1)} %collective-permute-done.up), channel_id=1, source_target_pairs={{0,1},{1,0},{2,3},{3,2},{4,5},{5,4},{6,7},{7,6},{8,9},{9,8},{10,11... | collective-permute-start | bytes 1597448 | tf_op jit(solution)/shard_map/ppermute | solution.py:210
  46.3 0.8 %copy-start.1 = (bf16[1040,256]{1,0:T(8,128)(2,1)}, bf16[1040,256]{1,0:T(8,128)(2,1)S(1)}, u32[]{:S(2)}) copy-start(bf16[1040,256]{1,0:T(8,128)(2,1)S(1)} %collective-permute-done.3.own_n) | copy-start | bytes 1597444
  46.3 1.0 %copy-start.4 = (bf16[1040,256]{1,0:T(8,128)(2,1)}, bf16[1040,256]{1,0:T(8,128)(2,1)S(1)}, u32[]{:S(2)}) copy-start(bf16[1040,256]{1,0:T(8,128)(2,1)S(1)} %collective-permute-done.4.dn_n) | copy-start | bytes 1597444
  47.3 0.8 %copy-start.5 = (bf16[1040,256]{1,0:T(8,128)(2,1)}, bf16[1040,256]{1,0:T(8,128)(2,1)S(1)}, u32[]{:S(2)}) copy-start(bf16[1040,256]{1,0:T(8,128)(2,1)S(1)} %collective-permute-done.2.up_n) | copy-start | bytes 1597444

commit v2 on v1

v2 whole, which is shorter than its diff:
```python
import jax
import jax.numpy as jnp
from jax import lax
from jax.experimental import pallas as pl
from jax.experimental.pallas import tpu as pltpu
from jax.sharding import PartitionSpec as P

G = 16
DB = 128
NBLK = 2
TILE = 64
TAPS = 17
STEP1 = 6
STEP2 = 8
PAIR = 2 * G
BF = jnp.bfloat16
F32 = jnp.float32
NT = (((1,), (1,)), ((), ()))
VMEM = pl.BlockSpec(memory_space=pltpu.VMEM)
SMEM = pl.BlockSpec(memory_space=pltpu.SMEM)
HBM = pl.BlockSpec(memory_space=pl.ANY)
LIMIT = pltpu.CompilerParams(vmem_limit_bytes=36 * 1024 * 1024)


def cost(us):
    return pl.CostEstimate(flops=us * 10**9, bytes_accessed=us * 10**6, transcendentals=0)


def iota(shape, dim):
    return lax.broadcasted_iota(jnp.int32, shape, dim)


def place():
    row, col = lax.axis_index("rows"), lax.axis_index("cols")
    rows, cols = lax.axis_size("rows"), lax.axis_size("cols")
    return col == 0, col == cols - 1, row == 0, row == rows - 1, row % 2


def pack_kernel(left, right, block_list, block_count, p0, p1, sems):
    cols = left.shape[1]
    copies = []
    for c, p in enumerate((p0, p1)):
        for i, src in enumerate((left, right)):
            dst = p.at[pl.ds(i * cols, cols), :]
            copies.append(pltpu.make_async_copy(src.at[c], dst, sems.at[2 * c + i]))
            copies[-1].start()
    ndisp = p0.shape[1]
    lane_block = (ndisp - 1 - iota((TILE // 16, ndisp), 1)) // DB
    lines = []
    for tile in range(cols // TILE):
        line = jnp.zeros(lane_block.shape, F32)
        for slot in range(block_list.shape[1]):
            listed = jnp.where(slot < block_count[0, tile], block_list[0, slot, tile], -1)
            line = jnp.where(lane_block == listed, 1.0, line)
        lines.append(line)
    lines = jnp.concatenate(lines, axis=0).astype(BF)
    for p in (p0, p1):
        p[2 * cols :, :] = lines
    for copy in copies:
        copy.wait()


def correlate(bands, nears, left_zero, corr):
    is_left, is_right, _, _, _ = place()
    cols, channels = left_zero.shape
    ndisp = corr.shape[2]
    group_of = iota((G, channels), 1) // (channels // G)
    gmask = jnp.where(group_of == iota((G, channels), 0), (channels // G) ** -0.5, 0.0).astype(F32)
    lane = iota((G, ndisp), 1)

    def spread(lines):
        lines = lines.astype(F32)
        return jnp.concatenate(
            [(lines[i : i + 1, :] * gmask).astype(BF) for i in range(lines.shape[0])], axis=0
        )

    for c, (xs, xn) in enumerate(zip(bands, nears)):

        def put(xx, value, c=c):
            corr[xx, c * G : c * G + G, :] = value.astype(BF)

        right = slice(cols, 2 * cols)
        near = xn[right, :]
        left_zero[...] = jnp.where(is_left, jnp.zeros_like(near), near)
        masks = xs[2 * cols : 2 * cols + 16, :].astype(F32)
        for k in range(cols // 16):
            x0 = k * 16
            a = spread(xs[x0 : x0 + 16, :])
            hi = lax.dot_general(a, xs[right, :], NT, preferred_element_type=F32)
            lo = lax.dot_general(a, left_zero[...], NT, preferred_element_type=F32)
            m = masks[k : k + 1]
            for i in range(16):
                x = x0 + i
                s = jnp.where(lane <= x, hi[i * G : i * G + G], lo[i * G : i * G + G])
                if x < ndisp - 1:
                    s = pltpu.roll(s, ndisp - 1 - x, 1)
                put(x + 2, s * m)

        mask_n = xn[2 * cols : 2 * cols + 16, :].astype(F32)
        tail = xn[cols - 16 : cols, :].astype(F32)[14:16]
        head = xn[0:16, :].astype(F32)[0:2]
        a = spread(jnp.concatenate([tail, head], axis=0))
        p_n = lax.dot_general(a, xn[right, :], NT, preferred_element_type=F32)
        p_o = lax.dot_general(a, xs[right, :], NT, preferred_element_type=F32)
        m_l = jnp.where(is_left, 0.0, mask_n[15:16])
        m_r = jnp.where(is_right, 0.0, mask_n[0:1])
        s = jnp.where(lane <= ndisp - 2, p_n[0:G], 0.0)
        put(0, pltpu.roll(s, 1, 1) * m_l)
        put(1, p_n[G : 2 * G] * m_l)
        s = jnp.where(lane <= 0, p_n[2 * G : 3 * G], p_o[2 * G : 3 * G])
        put(cols + 2, pltpu.roll(s, ndisp - 1, 1) * m_r)
        s = jnp.where(lane <= 1, p_n[3 * G : 4 * G], p_o[3 * G : 4 * G])
        put(cols + 3, pltpu.roll(s, ndisp - 2, 1) * m_r)


def first_conv(w_own, w_other, own, other, hidden):
    ndisp = own.shape[2]

    def step(s, carry):
        span = pl.ds(s * STEP1, STEP1 + 2)
        depth = (STEP1 + 2) * PAIR
        h = jnp.dot(w_own, own[span].reshape(depth, ndisp), preferred_element_type=F32)
        h += jnp.dot(w_other, other[span].reshape(depth, ndisp), preferred_element_type=F32)
        h = jnp.maximum(h, 0.0).astype(BF)
        hidden[pl.ds(s * STEP1, STEP1)] = h.reshape(STEP1, PAIR, ndisp)
        return carry

    lax.fori_loop(0, hidden.shape[0] // STEP1, step, 0, unroll=8)


def clear_rim(ref, outside, cols):
    is_left, is_right, _, _, _ = place()
    ndisp = ref.shape[2]
    for which in (0, 1):
        @pl.when(outside[which])
        def _():
            def clear(i, carry):
                ref[i, which * G : which * G + G, :] = jnp.zeros((G, ndisp), BF)
                return carry

            lax.fori_loop(0, cols + 2, clear, 0, unroll=8)

    for flag, col in ((is_left, 0), (is_right, cols + 1)):
        @pl.when(flag)
        def _():
            ref[col] = jnp.zeros((PAIR, ndisp), BF)


def tap_row(weights, width):
    pieces = []
    for j in range(3):
        for i in range(3):
            pieces.append(weights[i, j].astype(F32))
        pieces.append(jnp.zeros((G, G), F32))
    pieces.append(jnp.zeros((G, width - 12 * G), F32))
    return jnp.concatenate(pieces, axis=1)


def moved(line, by):
    return (pltpu.roll(line, by, 1) if by else line).astype(BF)


def permuted_columns(matrix, source):
    order = jnp.where(iota(source.shape, 0) == source, 1.0, 0.0).astype(BF)
    return jnp.dot(matrix, order, preferred_element_type=F32).astype(BF)


def weights_kernel(s1, s2, taps, w1, w2, tm):
    ndisp = tm.shape[1]
    depth = (STEP1 + 2) * 4 * G
    line = tap_row(s1, depth)
    plain = [moved(line, (xo * 4 + yo) * G) for xo in range(STEP1) for yo in range(2)]
    c = iota((depth, depth), 1)
    half = depth // 2
    source = ((c % half) // PAIR) * (2 * PAIR) + (c // half) * PAIR + c % PAIR
    sorted_cols = permuted_columns(jnp.concatenate(plain, axis=0), source)
    w1[0] = sorted_cols[:, :half]
    w1[1] = sorted_cols[:, half:]

    line = tap_row(s2, w2.shape[2])
    plain = [moved(line, (xo * 4 + yo) * G) for yo in range(2) for xo in range(STEP2)]
    size = 2 * STEP2 * G
    r = iota((size, size), 0)
    half = STEP2 * G
    source = (r // half) * half + (r % STEP2) * G + (r // STEP2) % G
    order = jnp.where(iota((size, size), 1) == source, 1.0, 0.0).astype(BF)
    plain = jnp.concatenate(plain, axis=0)
    plain = jnp.dot(order, plain, preferred_element_type=F32).astype(BF)
    w2[0] = plain
    c = iota((w2.shape[2], w2.shape[2]), 1)
    w2[1] = permuted_columns(plain, c + PAIR - 2 * PAIR * ((c // PAIR) % 2))

    k = iota((TAPS, ndisp), 0)
    at = iota((TAPS, ndisp), 1)
    spot = TAPS // 2 - k
    spot = jnp.where(spot < 0, spot + ndisp, spot)
    spot = jnp.where(at == spot, 1.0, 0.0).astype(BF)
    lines = jnp.dot(taps[...], spot, preferred_element_type=F32)
    r = iota((ndisp, ndisp), 0)
    c = iota((ndisp, ndisp), 1)
    flip = jnp.where(r + c == ndisp - 1, 1.0, 0.0).astype(BF)
    inside = jnp.abs(r - c) <= TAPS // 2
    for g in range(G):
        line = jnp.broadcast_to(lines[g : g + 1, :], (ndisp, ndisp))
        line = pltpu.roll(line, 0, 1, stride=1, stride_axis=0)
        line = jnp.where(inside, line, 0.0).astype(BF)
        tm[g * ndisp : (g + 1) * ndisp, :] = jnp.dot(
            flip, line, preferred_element_type=F32
        ).astype(BF)


def own_kernel(p0, p1, n0, n1, corr, left_zero):
    correlate((p0, p1), (n0, n1), left_zero, corr)


def partner_kernel(p0, p1, n0, n1, own, w1, hidden, left_zero, corr):
    _, _, first, last, odd = place()
    correlate((p0, p1), (n0, n1), left_zero, corr)
    first_conv(w1[odd], w1[1 - odd], own, corr, hidden)
    clear_rim(hidden, ((odd == 1) & first, (odd == 0) & last), left_zero.shape[0])


def last_kernel(
    p0, p1, n0, n1, own, partner, w1, w2, tm, out_ref, left_zero, corr, hidden, second
):
    _, _, first, last, odd = place()
    cols = left_zero.shape[0]
    ndisp = tm.shape[1]
    correlate((p0, p1), (n0, n1), left_zero, corr)
    first_conv(w1[1 - odd], w1[odd], own, corr, hidden)
    clear_rim(hidden, ((odd == 0) & first, (odd == 1) & last), cols)
    weights = w2[odd]

    def next_hidden(u, carry):
        halves = []
        for v in range(2):
            span = pl.ds((2 * u + v) * STEP2, STEP2 + 2)
            data = jnp.concatenate([hidden[span], partner[span]], axis=1)
            data = data.reshape((STEP2 + 2) * 2 * PAIR, ndisp)
            h = jnp.dot(weights, data, preferred_element_type=F32)
            halves.append(jnp.maximum(h, 0.0))
        for y in range(2):
            for o in range(G):
                r = (y * G + o) * STEP2
                both = jnp.concatenate([h[r : r + STEP2] for h in halves], axis=0)
                second[y, pl.ds(pl.multiple_of(u * 16, 16), 16), o * ndisp : (o + 1) * ndisp] = (
                    both.astype(BF)
                )
        return carry

    lax.fori_loop(0, cols // 16, next_hidden, 0, unroll=4)

    for y in range(2):
        out_ref[y] = jnp.dot(second[y], tm[...], preferred_element_type=F32)


def body(
    left_feat, right_feat, block_list, block_count, spatial_first, spatial_second, disparity_weight
):
    row_count, cols, channels = left_feat.shape
    ndisp = NBLK * DB
    bands = lax.axis_size("rows")
    row = lax.axis_index("rows")
    packed = jax.ShapeDtypeStruct((2 * cols + 16, channels), BF)
    chunks = pl.pallas_call(
        pack_kernel,
        out_shape=[packed, packed],
        in_specs=[HBM, HBM, SMEM, SMEM],
        out_specs=[VMEM, VMEM],
        scratch_shapes=[pltpu.SemaphoreType.DMA((4,))],
        cost_estimate=cost(1),
    )(left_feat, right_feat, block_list.transpose(0, 2, 1), block_count)

    partners = [(i, i ^ 1) for i in range(bands) if i ^ 1 < bands]
    onward = [(i, i + 2 - 4 * (i % 2)) for i in range(bands)]
    onward = [(i, j) for i, j in onward if 0 <= j < bands]
    across = [(0, 1), (1, 0)]

    def cross(x):
        return lax.ppermute(x, "cols", across)

    own_n = [cross(x) for x in chunks]
    by_partner = [lax.ppermute(x, "rows", partners) for x in chunks]
    steps1 = -(-(cols + 2) // STEP1)
    depth1 = (STEP1 + 2) * PAIR
    depth2 = (STEP2 + 2) * 2 * PAIR
    volume = (steps1 * STEP1 + 2, PAIR, ndisp)
    pair = (steps1 * STEP1, PAIR, ndisp)
    left_zero = pltpu.VMEM((cols, channels), BF)

    w1, w2, tm = pl.pallas_call(
        weights_kernel,
        out_shape=[
            jax.ShapeDtypeStruct((2, STEP1 * PAIR, depth1), BF),
            jax.ShapeDtypeStruct((2, STEP2 * PAIR, depth2), BF),
            jax.ShapeDtypeStruct((G * ndisp, ndisp), BF),
        ],
        in_specs=[VMEM] * 3,
        out_specs=[VMEM] * 3,
        compiler_params=LIMIT,
        cost_estimate=cost(4),
    )(spatial_first, spatial_second, disparity_weight.T)

    by_partner[0], w1 = lax.optimization_barrier((by_partner[0], w1))
    by_partner[0], own_n[0] = lax.optimization_barrier((by_partner[0], own_n[0]))
    own = pl.pallas_call(
        own_kernel,
        out_shape=jax.ShapeDtypeStruct(volume, BF),
        in_specs=[VMEM] * 4,
        out_specs=VMEM,
        scratch_shapes=[left_zero],
        compiler_params=LIMIT,
        cost_estimate=cost(4),
    )(*chunks, *own_n)

    def onward_row(c, x):
        if bands % 2:
            x = jnp.where(row == bands - 1, chunks[c], x)
        return lax.ppermute(x, "rows", onward)

    if bands % 2:
        onward.append((bands - 1, bands - 2))
    by_far = [onward_row(0, by_partner[0])]
    by_far[0], own = lax.optimization_barrier((by_far[0], own))
    by_far[0], by_partner[1] = lax.optimization_barrier((by_far[0], by_partner[1]))
    by_far.append(onward_row(1, by_partner[1]))
    by_partner_n = [cross(x) for x in by_partner]
    hidden = pl.pallas_call(
        partner_kernel,
        out_shape=jax.ShapeDtypeStruct(pair, BF),
        in_specs=[VMEM] * 6,
        out_specs=VMEM,
        scratch_shapes=[left_zero, pltpu.VMEM(volume, BF)],
        compiler_params=LIMIT,
        cost_estimate=cost(8),
    )(*by_partner, *by_partner_n, own, w1)

    by_far[1], hidden = lax.optimization_barrier((by_far[1], hidden))
    by_far_n = [cross(x) for x in by_far]
    return pl.pallas_call(
        last_kernel,
        out_shape=jax.ShapeDtypeStruct((row_count, cols, ndisp), F32),
        in_specs=[VMEM] * 9,
        out_specs=VMEM,
        scratch_shapes=[
            left_zero,
            pltpu.VMEM(volume, BF),
            pltpu.VMEM(pair, BF),
            pltpu.VMEM((2, cols, G * ndisp), BF),
        ],
        compiler_params=LIMIT,
        cost_estimate=cost(12),
    )(*by_far, *by_far_n, own, hidden, w1, w2, tm)


def solution(mesh):
    in_specs = (
        P(("pairs", "rows"), "cols", None),
        P(("pairs", "rows"), "cols", None),
        P(("pairs", "rows"), "cols", None),
        P(("pairs", "rows"), "cols"),
        P(),
        P(),
        P(),
    )
    out_specs = P(("pairs", "rows"), "cols", None)
    return jax.shard_map(body, mesh=mesh, in_specs=in_specs, out_specs=out_specs, check_vma=False)
```

time: 73.9 us -> 46.5 us (0.63)
  other arithmetic: 16.4 us -> 0 us
  waiting for transfers between devices: 19.6 us -> 5.58 us
  starting transfers between devices: 6.95 us -> 12.8 us
  local copies, waits for them, and re-layouts: 4.87 us -> 2.23 us
    ppermute x5 -> x10, waiting for transfers between devices: 19.6 us -> 5.58 us  [the longest x2 3.04 us: body(): by_partner = [lax.ppermute(x, 'rows', partners) for x in chunks]]
    select_n x1 -> x0, other arithmetic: 11.9 us -> none  [banded(): out = jnp.where(tap == k, weights[k][:, None, None], out)]
    ppermute x5 -> x10, starting transfers between devices: 6.95 us -> 12.8 us  [the longest x2 8.42 us: onward_row(): return lax.ppermute(x, 'rows', onward)]
    slice x2 -> x0, local copies, waits for them, and re-layouts: 1.97 us -> none  [the longest x1 1.79 us: banded(): out = jnp.where(tap == k, weights[k][:, None, None], out)]
    convert_element_type x4 -> x0, other arithmetic: 1.95 us -> none  [the longest x2 1.22 us: tap_row(): return jnp.pad(taps, ((0, 0), (0, width - taps.shape[1]))).astype(F32)]
    concatenate x1 -> x0, other arithmetic: 1.08 us -> none  [body(): jnp.concatenate([left_feat.reshape(-1, channels), right_feat.reshape(-1,...]
    reduce_or x1 -> x0, other arithmetic: 0.76 us -> none  [tile_masks(): active = jnp.any(hits, axis=1)]
    unnamed x46 -> x10, local copies, waits for them, and re-layouts: 2.6 us -> 2.23 us
  transfers between devices with their start and end apart: 5 -> 10, of which waited for: 2 -> 3; matrix products, arithmetic and copies ran while one was open for 23% -> 0% of each run, Pallas kernels for 0% -> 23%
where the time goes in v2:
time: 46.5 us; the launch traced here: 46.1 us
  Pallas kernels  25.5 us (55%)
  starting transfers between devices  12.8 us (28%)
  waiting for transfers between devices  5.58 us (12%)
  local copies, waits for them, and re-layouts  2.23 us (5%)
    pallas_call x1, Pallas kernels, body(): pl.pallas_call(last_kernel, out_shape=jax.ShapeDtypeStruct((row_count, co...  12.4 us
    ppermute x2, starting transfers between devices, onward_row(): return lax.ppermute(x, 'rows', onward)  8.42 us
    pallas_call x1, Pallas kernels, body(): pl.pallas_call(partner_kernel, out_shape=jax.ShapeDtypeStruct(pair, BF),...  6.21 us
    ppermute x2, starting transfers between devices, body(): by_partner = [lax.ppermute(x, 'rows', partners) for x in chunks]  3.11 us
    ppermute x2, waiting for transfers between devices, body(): by_partner = [lax.ppermute(x, 'rows', partners) for x in chunks]  3.04 us
    pallas_call x1, Pallas kernels, body(): pl.pallas_call(pack_kernel, out_shape=[packed, packed], in_specs=[HBM, HB...  2.6 us
    pallas_call x1, Pallas kernels, body(): pl.pallas_call(own_kernel, out_shape=jax.ShapeDtypeStruct(volume, BF), in...  2.57 us
    unnamed x10, local copies, waits for them, and re-layouts  2.23 us
  transfers between devices with their start and end apart: 10, of which 3 were waited for; matrix products, arithmetic and copies ran while one was open for 0% of the time, Pallas kernels for 23%

profile of v2, /device:TPU:0, one launch (start us, length us, event | category | flops | bytes accessed | tf_op | source)
XLA Modules:
  0.0 46.1 jit_solution(353959694455219975)
XLA Ops:
  0.0 2.6 %shard_map.73 = (bf16[528,256]{1,0:T(8,128)(2,1)}, bf16[528,256]{1,0:T(8,128)(2,1)}) custom-call(bf16[2,256,256]{2,1,0:T(8,128)(2,1)} %left.1, bf16[2,256,256]{2,1,0:T(8,128)(2,1)} %right.1, s32[1,2,4]{2,1,0:T(2,128)} %bitcast.3, s32[1,4]{1,0:T(1,128)} %block_count.1), custom_call_target="tpu_custom_call" | custom-call | flops 1000000000 | bytes 1000000 | tf_op jit(solution)/shard_map/pallas_call | solution.py:265
  2.6 3.0 %collective-permute-start = (bf16[528,256]{1,0:T(8,128)(2,1)}, bf16[528,256]{1,0:T(8,128)(2,1)S(1)}, u32[]{:S(2)}, u32[]{:S(2)}) collective-permute-start(bf16[528,256]{1,0:T(8,128)(2,1)} %get-tuple-element.20.p0), channel_id=1, source_target_pairs={{0,2},{2,0},{4,6},{6,4},{8,10},{10,8},{12,14},{14,12},{1,3},{3,1},... | collective-permute-start | bytes 811016 | tf_op jit(solution)/shard_map/ppermute | solution.py:283
  5.6 0.0 collective-permute-start.1
  5.6 0.5 %collective-permute-start.3 = (bf16[528,256]{1,0:T(8,128)(2,1)}, bf16[528,256]{1,0:T(8,128)(2,1)S(1)}, u32[]{:S(2)}, u32[]{:S(2)}) collective-permute-start(bf16[528,256]{1,0:T(8,128)(2,1)} %get-tuple-element.24.p1), channel_id=1, source_target_pairs={{0,1},{1,0},{2,3},{3,2},{4,5},{5,4},{6,7},{7,6},{8,9},{9,8},{10,11... | collective-permute-start | bytes 811016 | tf_op jit(solution)/shard_map/ppermute | solution.py:280
  6.2 0.1 collective-permute-start.4
  6.2 0.0 copy-start.2
  6.2 0.8 %copy-done.2 = bf16[3,3,16,16]{3,2,1,0:T(8,128)(2,1)S(1)} copy-done((bf16[3,3,16,16]{3,2,1,0:T(8,128)(2,1)S(1)}, bf16[3,3,16,16]{3,2,1,0:T(8,128)(2,1)}, u32[]{:S(2)}) %copy-start.2) | copy-done | bytes 4632
  7.0 0.0 copy-start.3
  7.0 0.8 %copy-done.3 = bf16[3,3,16,16]{3,2,1,0:T(8,128)(2,1)S(1)} copy-done((bf16[3,3,16,16]{3,2,1,0:T(8,128)(2,1)S(1)}, bf16[3,3,16,16]{3,2,1,0:T(8,128)(2,1)}, u32[]{:S(2)}) %copy-start.3) | copy-done | bytes 4632
  7.8 0.0 copy-start.4
  7.8 0.7 %copy-done.4 = bf16[17,16]{0,1:T(8,128)(2,1)S(1)} copy-done((bf16[17,16]{0,1:T(8,128)(2,1)S(1)}, bf16[17,16]{0,1:T(8,128)(2,1)}, u32[]{:S(2)}) %copy-start.4) | copy-done | bytes 568
  8.5 0.0 copy-start
  8.5 0.0 copy-start.1
  8.5 1.7 %shard_map.74 = (bf16[2,192,256]{2,1,0:T(8,128)(2,1)S(1)}, bf16[2,256,640]{2,1,0:T(8,128)(2,1)S(1)}, bf16[4096,256]{1,0:T(8,128)(2,1)S(1)}) custom-call(bf16[3,3,16,16]{3,2,1,0:T(8,128)(2,1)S(1)} %copy-done.2, bf16[3,3,16,16]{3,2,1,0:T(8,128)(2,1)S(1)} %copy-done.3, bf16[16,17]{1,0:T(8,128)(2,1)S(1)} %bitcast.2), custom_call_target="tpu_custom_call" | custom-call | flops 4000000000 | bytes 4000000 | tf_op jit(solution)/shard_map/pallas_call | solution.py:291
  10.1 3.0 %collective-permute-done.p0 = bf16[528,256]{1,0:T(8,128)(2,1)S(1)} collective-permute-done((bf16[528,256]{1,0:T(8,128)(2,1)}, bf16[528,256]{1,0:T(8,128)(2,1)S(1)}, u32[]{:S(2)}, u32[]{:S(2)}) %collective-permute-start) | collective-permute-done | bytes 270368 | tf_op jit(solution)/shard_map/ppermute | solution.py:283
  13.2 0.0 collective-permute-done.1.n0
  13.2 4.0 %collective-permute-start.2 = (bf16[528,256]{1,0:T(8,128)(2,1)S(1)}, bf16[528,256]{1,0:T(8,128)(2,1)S(1)}, u32[]{:S(2)}, u32[]{:S(2)}) collective-permute-start(bf16[528,256]{1,0:T(8,128)(2,1)S(1)} %collective-permute-done.p0), channel_id=1, source_target_pairs={{0,4},{4,8},{6,2},{8,12},{10,6},{14,10},{1,5},{5,9},{7,3},{9,13},{... | collective-permute-start | bytes 811016 | tf_op jit(solution)/shard_map/ppermute | solution.py:319
  17.2 0.1 collective-permute-start.6
  17.3 0.0 collective-permute-done.3.n1
  17.3 0.0 copy-done
  17.3 0.0 copy-done.1
  17.3 2.6 %shard_map.75.own = bf16[260,32,256]{2,1,0:T(8,128)(2,1)S(1)} custom-call(bf16[528,256]{1,0:T(8,128)(2,1)S(1)} %copy-done.1, bf16[528,256]{1,0:T(8,128)(2,1)S(1)} %copy-done, bf16[528,256]{1,0:T(8,128)(2,1)S(1)} %collective-permute-done.1.n0, bf16[528,256]{1,0:T(8,128)(2,1)S(1)} %collective-permute-done.3.n1), custom_call_target="tpu_custom_call" | custom-call | flops 4000000000 | bytes 4000000 | tf_op jit(solution)/shard_map/pallas_call | solution.py:306
  19.9 1.3 %collective-permute-done.2.p0 = bf16[528,256]{1,0:T(8,128)(2,1)S(1)} collective-permute-done((bf16[528,256]{1,0:T(8,128)(2,1)S(1)}, bf16[528,256]{1,0:T(8,128)(2,1)S(1)}, u32[]{:S(2)}, u32[]{:S(2)}) %collective-permute-start.2) | collective-permute-done | bytes 270368 | tf_op jit(solution)/shard_map/ppermute | solution.py:319
  21.1 0.0 collective-permute-done.4.p1
  21.1 0.0 collective-permute-start.7
  21.1 4.4 %collective-permute-start.5 = (bf16[528,256]{1,0:T(8,128)(2,1)S(1)}, bf16[528,256]{1,0:T(8,128)(2,1)S(1)}, u32[]{:S(2)}, u32[]{:S(2)}) collective-permute-start(bf16[528,256]{1,0:T(8,128)(2,1)S(1)} %collective-permute-done.4.p1), channel_id=1, source_target_pairs={{0,4},{4,8},{6,2},{8,12},{10,6},{14,10},{1,5},{5,9},{7,3},{9,13},{... | collective-permute-start | bytes 811016 | tf_op jit(solution)/shard_map/ppermute | solution.py:319
  25.5 0.3 collective-permute-start.8
  25.8 0.0 collective-permute-done.6.n0
  25.8 0.0 collective-permute-done.7.n1
  25.8 6.2 %shard_map.76.partner = bf16[258,32,256]{2,1,0:T(8,128)(2,1)S(1)} custom-call(bf16[528,256]{1,0:T(8,128)(2,1)S(1)} %collective-permute-done.p0, bf16[528,256]{1,0:T(8,128)(2,1)S(1)} %collective-permute-done.4.p1, bf16[528,256]{1,0:T(8,128)(2,1)S(1)} %collective-permute-done.6.n0, bf16[528,256]{1,0:T(8,128)(2,1)S(1)} %collective-permute-done.7.n1, ...), custom_call_target="tpu_custom_call" | custom-call | flops 8000000000 | bytes 8000000 | tf_op jit(solution)/shard_map/pallas_call | solution.py:328
  32.1 0.0 collective-permute-done.5.p1
  32.1 0.3 collective-permute-start.9
  32.4 0.0 collective-permute-done.8.n0
  32.4 1.3 %collective-permute-done.9.n1 = bf16[528,256]{1,0:T(8,128)(2,1)S(1)} collective-permute-done((bf16[528,256]{1,0:T(8,128)(2,1)S(1)}, bf16[528,256]{1,0:T(8,128)(2,1)S(1)}, u32[]{:S(2)}, u32[]{:S(2)}) %collective-permute-start.9) | collective-permute-done | bytes 270368 | tf_op jit(solution)/shard_map/ppermute | solution.py:280
  33.7 12.4 %shard_map.77 = f32[2,256,256]{2,1,0:T(8,128)} custom-call(bf16[528,256]{1,0:T(8,128)(2,1)S(1)} %collective-permute-done.2.p0, bf16[528,256]{1,0:T(8,128)(2,1)S(1)} %collective-permute-done.5.p1, bf16[528,256]{1,0:T(8,128)(2,1)S(1)} %collective-permute-done.8.n0, bf16[528,256]{1,0:T(8,128)(2,1)S(1)} %collective-permute-done.9.n1, ...), custom_call_target="tpu_custom_call" | custom-call | flops 12000000000 | bytes 12000000 | tf_op jit(solution)/shard_map/pallas_call | solution.py:340
Async XLA Ops:
  2.6 10.6 %collective-permute-start = (bf16[528,256]{1,0:T(8,128)(2,1)}, bf16[528,256]{1,0:T(8,128)(2,1)S(1)}, u32[]{:S(2)}, u32[]{:S(2)}) collective-permute-start(bf16[528,256]{1,0:T(8,128)(2,1)} %get-tuple-element.20.p0), channel_id=1, source_target_pairs={{0,2},{2,0},{4,6},{6,4},{8,10},{10,8},{12,14},{14,12},{1,3},{3,1},... | collective-permute-start | bytes 811016 | tf_op jit(solution)/shard_map/ppermute | solution.py:283
  5.6 7.5 %collective-permute-start.1 = (bf16[528,256]{1,0:T(8,128)(2,1)}, bf16[528,256]{1,0:T(8,128)(2,1)S(1)}, u32[]{:S(2)}, u32[]{:S(2)}) collective-permute-start(bf16[528,256]{1,0:T(8,128)(2,1)} %get-tuple-element.20.p0), channel_id=1, source_target_pairs={{0,1},{1,0},{2,3},{3,2},{4,5},{5,4},{6,7},{7,6},{8,9},{9,8},{10,11... | collective-permute-start | bytes 811016 | tf_op jit(solution)/shard_map/ppermute | solution.py:280
  5.6 11.6 %collective-permute-start.3 = (bf16[528,256]{1,0:T(8,128)(2,1)}, bf16[528,256]{1,0:T(8,128)(2,1)S(1)}, u32[]{:S(2)}, u32[]{:S(2)}) collective-permute-start(bf16[528,256]{1,0:T(8,128)(2,1)} %get-tuple-element.24.p1), channel_id=1, source_target_pairs={{0,1},{1,0},{2,3},{3,2},{4,5},{5,4},{6,7},{7,6},{8,9},{9,8},{10,11... | collective-permute-start | bytes 811016 | tf_op jit(solution)/shard_map/ppermute | solution.py:280
  6.2 15.0 %collective-permute-start.4 = (bf16[528,256]{1,0:T(8,128)(2,1)}, bf16[528,256]{1,0:T(8,128)(2,1)S(1)}, u32[]{:S(2)}, u32[]{:S(2)}) collective-permute-start(bf16[528,256]{1,0:T(8,128)(2,1)} %get-tuple-element.24.p1), channel_id=1, source_target_pairs={{0,2},{2,0},{4,6},{6,4},{8,10},{10,8},{12,14},{14,12},{1,3},{3,1},... | collective-permute-start | bytes 811016 | tf_op jit(solution)/shard_map/ppermute | solution.py:283
  6.2 0.8 %copy-start.2 = (bf16[3,3,16,16]{3,2,1,0:T(8,128)(2,1)S(1)}, bf16[3,3,16,16]{3,2,1,0:T(8,128)(2,1)}, u32[]{:S(2)}) copy-start(bf16[3,3,16,16]{3,2,1,0:T(8,128)(2,1)} %s1_.1) | copy-start | bytes 13828
  7.0 0.8 %copy-start.3 = (bf16[3,3,16,16]{3,2,1,0:T(8,128)(2,1)S(1)}, bf16[3,3,16,16]{3,2,1,0:T(8,128)(2,1)}, u32[]{:S(2)}) copy-start(bf16[3,3,16,16]{3,2,1,0:T(8,128)(2,1)} %s2_.1) | copy-start | bytes 13828
  7.8 0.7 %copy-start.4 = (bf16[17,16]{0,1:T(8,128)(2,1)S(1)}, bf16[17,16]{0,1:T(8,128)(2,1)}, u32[]{:S(2)}) copy-start(bf16[17,16]{0,1:T(8,128)(2,1)} %param.13) | copy-start | bytes 1636
  8.5 8.8 %copy-start = (bf16[528,256]{1,0:T(8,128)(2,1)S(1)}, bf16[528,256]{1,0:T(8,128)(2,1)}, u32[]{:S(2)}) copy-start(bf16[528,256]{1,0:T(8,128)(2,1)} %get-tuple-element.24.p1) | copy-start | bytes 811012
  8.5 8.8 %copy-start.1 = (bf16[528,256]{1,0:T(8,128)(2,1)S(1)}, bf16[528,256]{1,0:T(8,128)(2,1)}, u32[]{:S(2)}) copy-start(bf16[528,256]{1,0:T(8,128)(2,1)} %get-tuple-element.20.p0) | copy-start | bytes 811012
  13.2 8.0 %collective-permute-start.2 = (bf16[528,256]{1,0:T(8,128)(2,1)S(1)}, bf16[528,256]{1,0:T(8,128)(2,1)S(1)}, u32[]{:S(2)}, u32[]{:S(2)}) collective-permute-start(bf16[528,256]{1,0:T(8,128)(2,1)S(1)} %collective-permute-done.p0), channel_id=1, source_target_pairs={{0,4},{4,8},{6,2},{8,12},{10,6},{14,10},{1,5},{5,9},{7,3},{9,13},{... | collective-permute-start | bytes 811016 | tf_op jit(solution)/shard_map/ppermute | solution.py:319
  17.2 8.6 %collective-permute-start.6 = (bf16[528,256]{1,0:T(8,128)(2,1)S(1)}, bf16[528,256]{1,0:T(8,128)(2,1)S(1)}, u32[]{:S(2)}, u32[]{:S(2)}) collective-permute-start(bf16[528,256]{1,0:T(8,128)(2,1)S(1)} %collective-permute-done.p0), channel_id=1, source_target_pairs={{0,1},{1,0},{2,3},{3,2},{4,5},{5,4},{6,7},{7,6},{8,9},{9,8},{10,11... | collective-permute-start | bytes 811016 | tf_op jit(solution)/shard_map/ppermute | solution.py:280
  21.1 4.7 %collective-permute-start.7 = (bf16[528,256]{1,0:T(8,128)(2,1)S(1)}, bf16[528,256]{1,0:T(8,128)(2,1)S(1)}, u32[]{:S(2)}, u32[]{:S(2)}) collective-permute-start(bf16[528,256]{1,0:T(8,128)(2,1)S(1)} %collective-permute-done.4.p1), channel_id=1, source_target_pairs={{0,1},{1,0},{2,3},{3,2},{4,5},{5,4},{6,7},{7,6},{8,9},{9,8},{10,11... | collective-permute-start | bytes 811016 | tf_op jit(solution)/shard_map/ppermute | solution.py:280
  21.1 10.9 %collective-permute-start.5 = (bf16[528,256]{1,0:T(8,128)(2,1)S(1)}, bf16[528,256]{1,0:T(8,128)(2,1)S(1)}, u32[]{:S(2)}, u32[]{:S(2)}) collective-permute-start(bf16[528,256]{1,0:T(8,128)(2,1)S(1)} %collective-permute-done.4.p1), channel_id=1, source_target_pairs={{0,4},{4,8},{6,2},{8,12},{10,6},{14,10},{1,5},{5,9},{7,3},{9,13},{... | collective-permute-start | bytes 811016 | tf_op jit(solution)/shard_map/ppermute | solution.py:319
  25.5 6.9 %collective-permute-start.8 = (bf16[528,256]{1,0:T(8,128)(2,1)S(1)}, bf16[528,256]{1,0:T(8,128)(2,1)S(1)}, u32[]{:S(2)}, u32[]{:S(2)}) collective-permute-start(bf16[528,256]{1,0:T(8,128)(2,1)S(1)} %collective-permute-done.2.p0), channel_id=1, source_target_pairs={{0,1},{1,0},{2,3},{3,2},{4,5},{5,4},{6,7},{7,6},{8,9},{9,8},{10,11... | collective-permute-start | bytes 811016 | tf_op jit(solution)/shard_map/ppermute | solution.py:280
  32.1 1.6 %collective-permute-start.9 = (bf16[528,256]{1,0:T(8,128)(2,1)S(1)}, bf16[528,256]{1,0:T(8,128)(2,1)S(1)}, u32[]{:S(2)}, u32[]{:S(2)}) collective-permute-start(bf16[528,256]{1,0:T(8,128)(2,1)S(1)} %collective-permute-done.5.p1), channel_id=1, source_target_pairs={{0,1},{1,0},{2,3},{3,2},{4,5},{5,4},{6,7},{7,6},{8,9},{9,8},{10,11... | collective-permute-start | bytes 811016 | tf_op jit(solution)/shard_map/ppermute | solution.py:280

commit v3 on v2

--- a/solution.py
+++ b/solution.py
@@ -60,10 +60,10 @@
         copy.wait()
 
 
-def correlate(bands, nears, left_zero, corr):
+def correlate(rows, left_zero):
     is_left, is_right, _, _, _ = place()
     cols, channels = left_zero.shape
-    ndisp = corr.shape[2]
+    ndisp = NBLK * DB
     group_of = iota((G, channels), 1) // (channels // G)
     gmask = jnp.where(group_of == iota((G, channels), 0), (channels // G) ** -0.5, 0.0).astype(F32)
     lane = iota((G, ndisp), 1)
@@ -74,10 +74,10 @@
             [(lines[i : i + 1, :] * gmask).astype(BF) for i in range(lines.shape[0])], axis=0
         )
 
-    for c, (xs, xn) in enumerate(zip(bands, nears)):
-
-        def put(xx, value, c=c):
-            corr[xx, c * G : c * G + G, :] = value.astype(BF)
+    for xs, xn, corr in rows:
+
+        def put(xx, value, corr=corr):
+            corr[xx] = value.astype(BF)
 
         right = slice(cols, 2 * cols)
         near = xn[right, :]
@@ -113,19 +113,21 @@
         put(cols + 3, pltpu.roll(s, ndisp - 2, 1) * m_r)
 
 
+def row_block(refs, span):
+    data = jnp.concatenate([ref[span] for ref in refs], axis=1)
+    return data.reshape(data.shape[0] * data.shape[1], data.shape[2])
+
+
 def first_conv(w_own, w_other, own, other, hidden):
-    ndisp = own.shape[2]
-
     def step(s, carry):
         span = pl.ds(s * STEP1, STEP1 + 2)
-        depth = (STEP1 + 2) * PAIR
-        h = jnp.dot(w_own, own[span].reshape(depth, ndisp), preferred_element_type=F32)
-        h += jnp.dot(w_other, other[span].reshape(depth, ndisp), preferred_element_type=F32)
+        h = jnp.dot(w_own, row_block(own, span), preferred_element_type=F32)
+        h += jnp.dot(w_other, row_block(other, span), preferred_element_type=F32)
         h = jnp.maximum(h, 0.0).astype(BF)
-        hidden[pl.ds(s * STEP1, STEP1)] = h.reshape(STEP1, PAIR, ndisp)
+        hidden[pl.ds(s * STEP1, STEP1)] = h.reshape(STEP1, PAIR, h.shape[1])
         return carry
 
-    lax.fori_loop(0, hidden.shape[0] // STEP1, step, 0, unroll=8)
+    lax.fori_loop(0, hidden.shape[0] // STEP1, step, 0, unroll=True)
 
 
 def clear_rim(ref, outside, cols):
@@ -146,13 +148,12 @@
             ref[col] = jnp.zeros((PAIR, ndisp), BF)
 
 
-def tap_row(weights, width):
+def tap_row(weights, order, width):
     pieces = []
     for j in range(3):
-        for i in range(3):
-            pieces.append(weights[i, j].astype(F32))
-        pieces.append(jnp.zeros((G, G), F32))
-    pieces.append(jnp.zeros((G, width - 12 * G), F32))
+        for i in order:
+            pieces.append(jnp.zeros((G, G), F32) if i is None else weights[i, j].astype(F32))
+    pieces.append(jnp.zeros((G, width - 3 * len(order) * G), F32))
     return jnp.concatenate(pieces, axis=1)
 
 
@@ -168,7 +169,7 @@
 def weights_kernel(s1, s2, taps, w1, w2, tm):
     ndisp = tm.shape[1]
     depth = (STEP1 + 2) * 4 * G
-    line = tap_row(s1, depth)
+    line = tap_row(s1, (0, 1, 2, None), depth)
     plain = [moved(line, (xo * 4 + yo) * G) for xo in range(STEP1) for yo in range(2)]
     c = iota((depth, depth), 1)
     half = depth // 2
@@ -177,18 +178,14 @@
     w1[0] = sorted_cols[:, :half]
     w1[1] = sorted_cols[:, half:]
 
-    line = tap_row(s2, w2.shape[2])
-    plain = [moved(line, (xo * 4 + yo) * G) for yo in range(2) for xo in range(STEP2)]
-    size = 2 * STEP2 * G
+    size = STEP2 * G
     r = iota((size, size), 0)
-    half = STEP2 * G
-    source = (r // half) * half + (r % STEP2) * G + (r // STEP2) % G
+    source = (r % STEP2) * G + r // STEP2
     order = jnp.where(iota((size, size), 1) == source, 1.0, 0.0).astype(BF)
-    plain = jnp.concatenate(plain, axis=0)
-    plain = jnp.dot(order, plain, preferred_element_type=F32).astype(BF)
-    w2[0] = plain
-    c = iota((w2.shape[2], w2.shape[2]), 1)
-    w2[1] = permuted_columns(plain, c + PAIR - 2 * PAIR * ((c // PAIR) % 2))
+    for v, taps_order in enumerate(((0, 1, 2), (1, 2, 0), (2, 0, 1))):
+        line = tap_row(s2, taps_order, w2.shape[2])
+        plain = jnp.concatenate([moved(line, xo * 3 * G) for xo in range(STEP2)], axis=0)
+        w2[v] = jnp.dot(order, plain, preferred_element_type=F32).astype(BF)
 
     k = iota((TAPS, ndisp), 0)
     at = iota((TAPS, ndisp), 1)
@@ -209,46 +206,53 @@
         ).astype(BF)
 
 
-def own_kernel(p0, p1, n0, n1, corr, left_zero):
-    correlate((p0, p1), (n0, n1), left_zero, corr)
-
-
-def partner_kernel(p0, p1, n0, n1, own, w1, hidden, left_zero, corr):
+def own_kernel(own0, own1, own0_n, own1_n, o0, o1, left_zero):
+    correlate(((own0, own0_n, o0), (own1, own1_n, o1)), left_zero)
+
+
+def partner_kernel(par0, par1, par0_n, par1_n, o0, o1, w1, hidden, left_zero, p0, p1):
     _, _, first, last, odd = place()
-    correlate((p0, p1), (n0, n1), left_zero, corr)
-    first_conv(w1[odd], w1[1 - odd], own, corr, hidden)
+    correlate(((par0, par0_n, p0), (par1, par1_n, p1)), left_zero)
+    first_conv(w1[odd], w1[1 - odd], (o0, o1), (p0, p1), hidden)
     clear_rim(hidden, ((odd == 1) & first, (odd == 0) & last), left_zero.shape[0])
 
 
+def row_kernel(xs, xn, corr, left_zero):
+    correlate(((xs, xn, corr),), left_zero)
+
+
 def last_kernel(
-    p0, p1, n0, n1, own, partner, w1, w2, tm, out_ref, left_zero, corr, hidden, second
+    far1, far1_n, f0, o0, o1, partner, w1, w2, tm, out_ref, left_zero, f1, hidden, second
 ):
     _, _, first, last, odd = place()
     cols = left_zero.shape[0]
     ndisp = tm.shape[1]
-    correlate((p0, p1), (n0, n1), left_zero, corr)
-    first_conv(w1[1 - odd], w1[odd], own, corr, hidden)
+    correlate(((far1, far1_n, f1),), left_zero)
+    first_conv(w1[1 - odd], w1[odd], (o0, o1), (f0, f1), hidden)
     clear_rim(hidden, ((odd == 0) & first, (odd == 1) & last), cols)
-    weights = w2[odd]
+    one = pl.ds(pl.multiple_of(odd * G, G), G)
+    other = pl.ds(pl.multiple_of((1 - odd) * G, G), G)
+    outputs = ((odd, w2[odd]), (1 - odd, w2[2 * odd]))
 
     def next_hidden(u, carry):
-        halves = []
+        halves = ([], [])
         for v in range(2):
             span = pl.ds((2 * u + v) * STEP2, STEP2 + 2)
-            data = jnp.concatenate([hidden[span], partner[span]], axis=1)
-            data = data.reshape((STEP2 + 2) * 2 * PAIR, ndisp)
-            h = jnp.dot(weights, data, preferred_element_type=F32)
-            halves.append(jnp.maximum(h, 0.0))
-        for y in range(2):
+            blocks = ((hidden[span], partner[span, one, :]), (hidden[span, other, :], partner[span]))
+            for half, block, (_, weights) in zip(halves, blocks, outputs):
+                data = jnp.concatenate(block, axis=1).reshape((STEP2 + 2) * 3 * G, ndisp)
+                h = jnp.dot(weights, data, preferred_element_type=F32)
+                half.append(jnp.maximum(h, 0.0))
+        for half, (y, _) in zip(halves, outputs):
             for o in range(G):
-                r = (y * G + o) * STEP2
-                both = jnp.concatenate([h[r : r + STEP2] for h in halves], axis=0)
+                r = o * STEP2
+                both = jnp.concatenate([h[r : r + STEP2] for h in half], axis=0)
                 second[y, pl.ds(pl.multiple_of(u * 16, 16), 16), o * ndisp : (o + 1) * ndisp] = (
                     both.astype(BF)
                 )
         return carry
 
-    lax.fori_loop(0, cols // 16, next_hidden, 0, unroll=4)
+    lax.fori_loop(0, cols // 16, next_hidden, 0, unroll=True)
 
     for y in range(2):
         out_ref[y] = jnp.dot(second[y], tm[...], preferred_element_type=F32)
@@ -279,12 +283,13 @@
     def cross(x):
         return lax.ppermute(x, "cols", across)
 
+    par0, par1 = [lax.ppermute(x, "rows", partners) for x in chunks]
     own_n = [cross(x) for x in chunks]
-    by_partner = [lax.ppermute(x, "rows", partners) for x in chunks]
     steps1 = -(-(cols + 2) // STEP1)
     depth1 = (STEP1 + 2) * PAIR
-    depth2 = (STEP2 + 2) * 2 * PAIR
-    volume = (steps1 * STEP1 + 2, PAIR, ndisp)
+    depth2 = (STEP2 + 2) * 3 * G
+    volume = (steps1 * STEP1 + 2, G, ndisp)
+    volume_out = jax.ShapeDtypeStruct(volume, BF)
     pair = (steps1 * STEP1, PAIR, ndisp)
     left_zero = pltpu.VMEM((cols, channels), BF)
 
@@ -292,7 +297,7 @@
         weights_kernel,
         out_shape=[
             jax.ShapeDtypeStruct((2, STEP1 * PAIR, depth1), BF),
-            jax.ShapeDtypeStruct((2, STEP2 * PAIR, depth2), BF),
+            jax.ShapeDtypeStruct((3, STEP2 * G, depth2), BF),
             jax.ShapeDtypeStruct((G * ndisp, ndisp), BF),
         ],
         in_specs=[VMEM] * 3,
@@ -301,42 +306,55 @@
         cost_estimate=cost(4),
     )(spatial_first, spatial_second, disparity_weight.T)
 
-    by_partner[0], w1 = lax.optimization_barrier((by_partner[0], w1))
-    by_partner[0], own_n[0] = lax.optimization_barrier((by_partner[0], own_n[0]))
-    own = pl.pallas_call(
+    par0, w1 = lax.optimization_barrier((par0, w1))
+    if bands % 2:
+        onward.append((bands - 1, bands - 2))
+
+    def send_on(chunk, x):
+        if bands % 2:
+            x = jnp.where(row == bands - 1, chunk, x)
+        return lax.ppermute(x, "rows", onward)
+
+    far0 = send_on(chunks[0], par0)
+    par0_n = cross(par0)
+
+    par0, own_n[0] = lax.optimization_barrier((par0, own_n[0]))
+    o0, o1 = pl.pallas_call(
         own_kernel,
-        out_shape=jax.ShapeDtypeStruct(volume, BF),
+        out_shape=[volume_out] * 2,
         in_specs=[VMEM] * 4,
-        out_specs=VMEM,
+        out_specs=[VMEM] * 2,
         scratch_shapes=[left_zero],
         compiler_params=LIMIT,
         cost_estimate=cost(4),
     )(*chunks, *own_n)
-
-    def onward_row(c, x):
-        if bands % 2:
-            x = jnp.where(row == bands - 1, chunks[c], x)
-        return lax.ppermute(x, "rows", onward)
-
-    if bands % 2:
-        onward.append((bands - 1, bands - 2))
-    by_far = [onward_row(0, by_partner[0])]
-    by_far[0], own = lax.optimization_barrier((by_far[0], own))
-    by_far[0], by_partner[1] = lax.optimization_barrier((by_far[0], by_partner[1]))
-    by_far.append(onward_row(1, by_partner[1]))
-    by_partner_n = [cross(x) for x in by_partner]
+    far0, o0 = lax.optimization_barrier((far0, o0))
+    par1, o1 = lax.optimization_barrier((par1, o1))
+    far1 = send_on(chunks[1], par1)
+    par1_n = cross(par1)
+    par1_n, far0 = lax.optimization_barrier((par1_n, far0))
+
     hidden = pl.pallas_call(
         partner_kernel,
         out_shape=jax.ShapeDtypeStruct(pair, BF),
-        in_specs=[VMEM] * 6,
+        in_specs=[VMEM] * 7,
         out_specs=VMEM,
-        scratch_shapes=[left_zero, pltpu.VMEM(volume, BF)],
+        scratch_shapes=[left_zero, pltpu.VMEM(volume, BF), pltpu.VMEM(volume, BF)],
         compiler_params=LIMIT,
         cost_estimate=cost(8),
-    )(*by_partner, *by_partner_n, own, w1)
-
-    by_far[1], hidden = lax.optimization_barrier((by_far[1], hidden))
-    by_far_n = [cross(x) for x in by_far]
+    )(par0, par1, par0_n, par1_n, o0, o1, w1)
+    far0_n = cross(far0)
+    far1, hidden = lax.optimization_barrier((far1, hidden))
+    f0 = pl.pallas_call(
+        row_kernel,
+        out_shape=volume_out,
+        in_specs=[VMEM] * 2,
+        out_specs=VMEM,
+        scratch_shapes=[left_zero],
+        compiler_params=LIMIT,
+        cost_estimate=cost(1),
+    )(far0, far0_n)
+
     return pl.pallas_call(
         last_kernel,
         out_shape=jax.ShapeDtypeStruct((row_count, cols, ndisp), F32),
@@ -350,7 +368,7 @@
         ],
         compiler_params=LIMIT,
         cost_estimate=cost(12),
-    )(*by_far, *by_far_n, own, hidden, w1, w2, tm)
+    )(far1, cross(far1), f0, o0, o1, hidden, w1, w2, tm)
 
 
 def solution(mesh):

time: 46.5 us -> 40.3 us (0.87)
  Pallas kernels: 25.5 us -> 21.9 us
  local copies, waits for them, and re-layouts: 2.23 us -> 0.02 us
  starting transfers between devices: 12.8 us -> 11.8 us
  waiting for transfers between devices: 5.58 us -> 6.28 us
    pallas_call x1, Pallas kernels: 12.4 us -> 8.54 us  [body(): pl.pallas_call(last_kernel, out_shape=jax.ShapeDtypeStruct((row_count, co...]
    unnamed x10, local copies, waits for them, and re-layouts: 2.23 us -> 0.02 us
    ppermute x4, waiting for transfers between devices: 4.31 us -> 6.12 us  [the longest x2 5.5 us: body(): par0, par1 = [lax.ppermute(x, 'rows', partners) for x in chunks]]
    pallas_call x1 -> x2, Pallas kernels: 2.57 us -> 3.96 us  [the longest x1 2.58 us: body(): pl.pallas_call(own_kernel, out_shape=[volume_out] * 2, in_specs=[VMEM] *...]
    ppermute x6, waiting for transfers between devices: 1.27 us -> 0.16 us  [cross(): return lax.ppermute(x, 'cols', across)]
    pallas_call x1, Pallas kernels: 6.21 us -> 5.21 us  [body(): pl.pallas_call(partner_kernel, out_shape=jax.ShapeDtypeStruct(pair, BF),...]
    ppermute x4, starting transfers between devices: 11.5 us -> 10.6 us  [the longest x2 7.49 us: send_on(): return lax.ppermute(x, 'rows', onward)]
  transfers between devices with their start and end apart: 10 -> 10, of which waited for: 3 -> 3; matrix products, arithmetic and copies ran while one was open for 0% -> 0% of each run, Pallas kernels for 23% -> 26%
where the time goes in v3:
time: 40.3 us; the launch traced here: 40 us
  Pallas kernels  21.9 us (54%)
  starting transfers between devices  11.8 us (29%)
  waiting for transfers between devices  6.28 us (16%)
    pallas_call x1, Pallas kernels, body(): pl.pallas_call(last_kernel, out_shape=jax.ShapeDtypeStruct((row_count, co...  8.54 us
    ppermute x2, starting transfers between devices, send_on(): return lax.ppermute(x, 'rows', onward)  7.49 us
    ppermute x2, waiting for transfers between devices, body(): par0, par1 = [lax.ppermute(x, 'rows', partners) for x in chunks]  5.5 us
    pallas_call x1, Pallas kernels, body(): pl.pallas_call(partner_kernel, out_shape=jax.ShapeDtypeStruct(pair, BF),...  5.21 us
    ppermute x2, starting transfers between devices, body(): par0, par1 = [lax.ppermute(x, 'rows', partners) for x in chunks]  3.11 us
    pallas_call x1, Pallas kernels, body(): pl.pallas_call(pack_kernel, out_shape=[packed, packed], in_specs=[HBM, HB...  2.73 us
    pallas_call x1, Pallas kernels, body(): pl.pallas_call(own_kernel, out_shape=[volume_out] * 2, in_specs=[VMEM] *...  2.58 us
    pallas_call x1, Pallas kernels, body(): pl.pallas_call(weights_kernel, out_shape=[jax.ShapeDtypeStruct((2, STEP1...  1.41 us
  transfers between devices with their start and end apart: 10, of which 3 were waited for; matrix products, arithmetic and copies ran while one was open for 0% of the time, Pallas kernels for 26%

profile of v3, /device:TPU:0, one launch (start us, length us, event | category | flops | bytes accessed | tf_op | source)
XLA Modules:
  0.0 40.0 jit_solution(1601988711809632115)
XLA Ops:
  0.0 0.0 copy-start.4
  0.0 0.0 copy-start.2
  0.0 0.0 copy-start.3
  0.0 2.7 %shard_map.73 = (bf16[528,256]{1,0:T(8,128)(2,1)}, bf16[528,256]{1,0:T(8,128)(2,1)}) custom-call(bf16[2,256,256]{2,1,0:T(8,128)(2,1)} %left.1, bf16[2,256,256]{2,1,0:T(8,128)(2,1)} %right.1, s32[1,2,4]{2,1,0:T(2,128)} %bitcast.3, s32[1,4]{1,0:T(1,128)} %block_count.1), custom_call_target="tpu_custom_call" | custom-call | flops 1000000000 | bytes 1000000 | tf_op jit(solution)/shard_map/pallas_call | solution.py:269
  2.7 3.0 %collective-permute-start.1 = (bf16[528,256]{1,0:T(8,128)(2,1)}, bf16[528,256]{1,0:T(8,128)(2,1)S(1)}, u32[]{:S(2)}, u32[]{:S(2)}) collective-permute-start(bf16[528,256]{1,0:T(8,128)(2,1)} %get-tuple-element.25.own0), channel_id=1, source_target_pairs={{0,2},{2,0},{4,6},{6,4},{8,10},{10,8},{12,14},{14,12},{1,3},{3,1},... | collective-permute-start | bytes 811016 | tf_op jit(solution)/shard_map/ppermute | solution.py:286
  5.8 0.0 collective-permute-start.2
  5.8 0.5 %collective-permute-start.3 = (bf16[528,256]{1,0:T(8,128)(2,1)}, bf16[528,256]{1,0:T(8,128)(2,1)S(1)}, u32[]{:S(2)}, u32[]{:S(2)}) collective-permute-start(bf16[528,256]{1,0:T(8,128)(2,1)} %get-tuple-element.24.own1), channel_id=1, source_target_pairs={{0,1},{1,0},{2,3},{3,2},{4,5},{5,4},{6,7},{7,6},{8,9},{9,8},{10,11... | collective-permute-start | bytes 811016 | tf_op jit(solution)/shard_map/ppermute | solution.py:284
  6.3 0.1 collective-permute-start
  6.4 0.0 copy-done.4
  6.4 0.0 copy-done.2
  6.4 0.0 copy-done.3
  6.4 0.0 copy-start
  6.4 0.0 copy-start.1
  6.4 1.4 %shard_map.74 = (bf16[2,192,256]{2,1,0:T(8,128)(2,1)S(1)}, bf16[3,128,480]{2,1,0:T(8,128)(2,1)S(1)}, bf16[4096,256]{1,0:T(8,128)(2,1)S(1)}) custom-call(bf16[3,3,16,16]{3,2,1,0:T(8,128)(2,1)S(1)} %copy-done.2, bf16[3,3,16,16]{3,2,1,0:T(8,128)(2,1)S(1)} %copy-done.3, bf16[16,17]{1,0:T(8,128)(2,1)S(1)} %bitcast.2), custom_call_target="tpu_custom_call" | custom-call | flops 4000000000 | bytes 4000000 | tf_op jit(solution)/shard_map/pallas_call | solution.py:296
  7.8 5.5 %collective-permute-done.1.par0 = bf16[528,256]{1,0:T(8,128)(2,1)S(1)} collective-permute-done((bf16[528,256]{1,0:T(8,128)(2,1)}, bf16[528,256]{1,0:T(8,128)(2,1)S(1)}, u32[]{:S(2)}, u32[]{:S(2)}) %collective-permute-start.1) | collective-permute-done | bytes 270368 | tf_op jit(solution)/shard_map/ppermute | solution.py:286
  13.3 4.0 %collective-permute-start.7 = (bf16[528,256]{1,0:T(8,128)(2,1)S(1)}, bf16[528,256]{1,0:T(8,128)(2,1)S(1)}, u32[]{:S(2)}, u32[]{:S(2)}) collective-permute-start(bf16[528,256]{1,0:T(8,128)(2,1)S(1)} %collective-permute-done.1.par0), channel_id=1, source_target_pairs={{0,4},{4,8},{6,2},{8,12},{10,6},{14,10},{1,5},{5,9},{7,3},{9,13},{... | collective-permute-start | bytes 811016 | tf_op jit(solution)/shard_map/ppermute | solution.py:316
  17.3 0.0 collective-permute-done.2.own0_n
  17.3 0.0 collective-permute-done.3.own1_n
  17.4 0.0 copy-done
  17.4 0.0 copy-done.1
  17.4 2.6 %shard_map.75 = (bf16[260,16,256]{2,1,0:T(8,128)(2,1)S(1)}, bf16[260,16,256]{2,1,0:T(8,128)(2,1)S(1)}) custom-call(bf16[528,256]{1,0:T(8,128)(2,1)S(1)} %copy-done.1, bf16[528,256]{1,0:T(8,128)(2,1)S(1)} %copy-done, bf16[528,256]{1,0:T(8,128)(2,1)S(1)} %collective-permute-done.2.own0_n, bf16[528,256]{1,0:T(8,128)(2,1)S(1)} %collective-permute-done.3.own1_n), custom_call_target="tpu_custom_call" | custom-call | flops 4000000000 | bytes 4000000 | tf_op jit(solution)/shard_map/pallas_call | solution.py:322
  20.0 0.0 collective-permute-done.par1
  20.0 0.1 collective-permute-start.6
  20.0 0.5 %collective-permute-start.5 = (bf16[528,256]{1,0:T(8,128)(2,1)S(1)}, bf16[528,256]{1,0:T(8,128)(2,1)S(1)}, u32[]{:S(2)}, u32[]{:S(2)}) collective-permute-start(bf16[528,256]{1,0:T(8,128)(2,1)S(1)} %collective-permute-done.1.par0), channel_id=1, source_target_pairs={{0,1},{1,0},{2,3},{3,2},{4,5},{5,4},{6,7},{7,6},{8,9},{9,8},{10,11... | collective-permute-start | bytes 811016 | tf_op jit(solution)/shard_map/ppermute | solution.py:284
  20.5 3.5 %collective-permute-start.4 = (bf16[528,256]{1,0:T(8,128)(2,1)S(1)}, bf16[528,256]{1,0:T(8,128)(2,1)S(1)}, u32[]{:S(2)}, u32[]{:S(2)}) collective-permute-start(bf16[528,256]{1,0:T(8,128)(2,1)S(1)} %collective-permute-done.par1), channel_id=1, source_target_pairs={{0,4},{4,8},{6,2},{8,12},{10,6},{14,10},{1,5},{5,9},{7,3},{9,13},{... | collective-permute-start | bytes 811016 | tf_op jit(solution)/shard_map/ppermute | solution.py:316
  24.0 0.0 collective-permute-done.7.xs
  24.0 0.0 collective-permute-done.6.par1_n
  24.0 0.1 collective-permute-start.9
  24.1 0.0 collective-permute-done.5.par0_n
  24.1 5.2 %shard_map.76.partner = bf16[258,32,256]{2,1,0:T(8,128)(2,1)S(1)} custom-call(bf16[528,256]{1,0:T(8,128)(2,1)S(1)} %collective-permute-done.1.par0, bf16[528,256]{1,0:T(8,128)(2,1)S(1)} %collective-permute-done.par1, bf16[528,256]{1,0:T(8,128)(2,1)S(1)} %collective-permute-done.5.par0_n, bf16[528,256]{1,0:T(8,128)(2,1)S(1)} %collective-permute-done.6.par1_n, ...), custom_call_target="tpu_custom_call" | custom-call | flops 8000000000 | bytes 8000000 | tf_op jit(solution)/shard_map/pallas_call | solution.py:337
  29.3 0.6 %collective-permute-done.4.far1 = bf16[528,256]{1,0:T(8,128)(2,1)S(1)} collective-permute-done((bf16[528,256]{1,0:T(8,128)(2,1)S(1)}, bf16[528,256]{1,0:T(8,128)(2,1)S(1)}, u32[]{:S(2)}, u32[]{:S(2)}) %collective-permute-start.4) | collective-permute-done | bytes 270368 | tf_op jit(solution)/shard_map/ppermute | solution.py:316
  30.0 0.0 collective-permute-start.8
  30.0 0.0 collective-permute-done.9.xn
  30.0 1.4 %shard_map.77.f0 = bf16[260,16,256]{2,1,0:T(8,128)(2,1)S(1)} custom-call(bf16[528,256]{1,0:T(8,128)(2,1)S(1)} %collective-permute-done.7.xs, bf16[528,256]{1,0:T(8,128)(2,1)S(1)} %collective-permute-done.9.xn), custom_call_target="tpu_custom_call" | custom-call | flops 1000000000 | bytes 1000000 | tf_op jit(solution)/shard_map/pallas_call | solution.py:348
  31.4 0.2 collective-permute-done.8.far1_n
  31.5 8.5 %shard_map.78 = f32[2,256,256]{2,1,0:T(8,128)} custom-call(bf16[528,256]{1,0:T(8,128)(2,1)S(1)} %collective-permute-done.4.far1, bf16[528,256]{1,0:T(8,128)(2,1)S(1)} %collective-permute-done.8.far1_n, bf16[260,16,256]{2,1,0:T(8,128)(2,1)S(1)} %shard_map.77.f0, bf16[260,16,256]{2,1,0:T(8,128)(2,1)S(1)} %get-tuple-element.35.o0, ...), custom_call_target="tpu_custom_call" | custom-call | flops 12000000000 | bytes 12000000 | tf_op jit(solution)/shard_map/pallas_call | solution.py:358
Async XLA Ops:
  0.0 6.4 %copy-start.4 = (bf16[17,16]{0,1:T(8,128)(2,1)S(1)}, bf16[17,16]{0,1:T(8,128)(2,1)}, u32[]{:S(2)}) copy-start(bf16[17,16]{0,1:T(8,128)(2,1)} %param.13) | copy-start | bytes 1636
  0.0 6.4 %copy-start.2 = (bf16[3,3,16,16]{3,2,1,0:T(8,128)(2,1)S(1)}, bf16[3,3,16,16]{3,2,1,0:T(8,128)(2,1)}, u32[]{:S(2)}) copy-start(bf16[3,3,16,16]{3,2,1,0:T(8,128)(2,1)} %s1_.1) | copy-start | bytes 13828
  0.0 6.4 %copy-start.3 = (bf16[3,3,16,16]{3,2,1,0:T(8,128)(2,1)S(1)}, bf16[3,3,16,16]{3,2,1,0:T(8,128)(2,1)}, u32[]{:S(2)}) copy-start(bf16[3,3,16,16]{3,2,1,0:T(8,128)(2,1)} %s2_.1) | copy-start | bytes 13828
  2.7 10.6 %collective-permute-start.1 = (bf16[528,256]{1,0:T(8,128)(2,1)}, bf16[528,256]{1,0:T(8,128)(2,1)S(1)}, u32[]{:S(2)}, u32[]{:S(2)}) collective-permute-start(bf16[528,256]{1,0:T(8,128)(2,1)} %get-tuple-element.25.own0), channel_id=1, source_target_pairs={{0,2},{2,0},{4,6},{6,4},{8,10},{10,8},{12,14},{14,12},{1,3},{3,1},... | collective-permute-start | bytes 811016 | tf_op jit(solution)/shard_map/ppermute | solution.py:286
  5.8 11.6 %collective-permute-start.2 = (bf16[528,256]{1,0:T(8,128)(2,1)}, bf16[528,256]{1,0:T(8,128)(2,1)S(1)}, u32[]{:S(2)}, u32[]{:S(2)}) collective-permute-start(bf16[528,256]{1,0:T(8,128)(2,1)} %get-tuple-element.25.own0), channel_id=1, source_target_pairs={{0,1},{1,0},{2,3},{3,2},{4,5},{5,4},{6,7},{7,6},{8,9},{9,8},{10,11... | collective-permute-start | bytes 811016 | tf_op jit(solution)/shard_map/ppermute | solution.py:284
  5.8 11.6 %collective-permute-start.3 = (bf16[528,256]{1,0:T(8,128)(2,1)}, bf16[528,256]{1,0:T(8,128)(2,1)S(1)}, u32[]{:S(2)}, u32[]{:S(2)}) collective-permute-start(bf16[528,256]{1,0:T(8,128)(2,1)} %get-tuple-element.24.own1), channel_id=1, source_target_pairs={{0,1},{1,0},{2,3},{3,2},{4,5},{5,4},{6,7},{7,6},{8,9},{9,8},{10,11... | collective-permute-start | bytes 811016 | tf_op jit(solution)/shard_map/ppermute | solution.py:284
  6.3 13.7 %collective-permute-start = (bf16[528,256]{1,0:T(8,128)(2,1)}, bf16[528,256]{1,0:T(8,128)(2,1)S(1)}, u32[]{:S(2)}, u32[]{:S(2)}) collective-permute-start(bf16[528,256]{1,0:T(8,128)(2,1)} %get-tuple-element.24.own1), channel_id=1, source_target_pairs={{0,2},{2,0},{4,6},{6,4},{8,10},{10,8},{12,14},{14,12},{1,3},{3,1},... | collective-permute-start | bytes 811016 | tf_op jit(solution)/shard_map/ppermute | solution.py:286
  6.4 11.0 %copy-start = (bf16[528,256]{1,0:T(8,128)(2,1)S(1)}, bf16[528,256]{1,0:T(8,128)(2,1)}, u32[]{:S(2)}) copy-start(bf16[528,256]{1,0:T(8,128)(2,1)} %get-tuple-element.24.own1) | copy-start | bytes 811012
  6.4 11.0 %copy-start.1 = (bf16[528,256]{1,0:T(8,128)(2,1)S(1)}, bf16[528,256]{1,0:T(8,128)(2,1)}, u32[]{:S(2)}) copy-start(bf16[528,256]{1,0:T(8,128)(2,1)} %get-tuple-element.25.own0) | copy-start | bytes 811012
  13.3 10.7 %collective-permute-start.7 = (bf16[528,256]{1,0:T(8,128)(2,1)S(1)}, bf16[528,256]{1,0:T(8,128)(2,1)S(1)}, u32[]{:S(2)}, u32[]{:S(2)}) collective-permute-start(bf16[528,256]{1,0:T(8,128)(2,1)S(1)} %collective-permute-done.1.par0), channel_id=1, source_target_pairs={{0,4},{4,8},{6,2},{8,12},{10,6},{14,10},{1,5},{5,9},{7,3},{9,13},{... | collective-permute-start | bytes 811016 | tf_op jit(solution)/shard_map/ppermute | solution.py:316
  20.0 4.1 %collective-permute-start.6 = (bf16[528,256]{1,0:T(8,128)(2,1)S(1)}, bf16[528,256]{1,0:T(8,128)(2,1)S(1)}, u32[]{:S(2)}, u32[]{:S(2)}) collective-permute-start(bf16[528,256]{1,0:T(8,128)(2,1)S(1)} %collective-permute-done.par1), channel_id=1, source_target_pairs={{0,1},{1,0},{2,3},{3,2},{4,5},{5,4},{6,7},{7,6},{8,9},{9,8},{10,11... | collective-permute-start | bytes 811016 | tf_op jit(solution)/shard_map/ppermute | solution.py:284
  20.0 4.1 %collective-permute-start.5 = (bf16[528,256]{1,0:T(8,128)(2,1)S(1)}, bf16[528,256]{1,0:T(8,128)(2,1)S(1)}, u32[]{:S(2)}, u32[]{:S(2)}) collective-permute-start(bf16[528,256]{1,0:T(8,128)(2,1)S(1)} %collective-permute-done.1.par0), channel_id=1, source_target_pairs={{0,1},{1,0},{2,3},{3,2},{4,5},{5,4},{6,7},{7,6},{8,9},{9,8},{10,11... | collective-permute-start | bytes 811016 | tf_op jit(solution)/shard_map/ppermute | solution.py:284
  20.5 9.4 %collective-permute-start.4 = (bf16[528,256]{1,0:T(8,128)(2,1)S(1)}, bf16[528,256]{1,0:T(8,128)(2,1)S(1)}, u32[]{:S(2)}, u32[]{:S(2)}) collective-permute-start(bf16[528,256]{1,0:T(8,128)(2,1)S(1)} %collective-permute-done.par1), channel_id=1, source_target_pairs={{0,4},{4,8},{6,2},{8,12},{10,6},{14,10},{1,5},{5,9},{7,3},{9,13},{... | collective-permute-start | bytes 811016 | tf_op jit(solution)/shard_map/ppermute | solution.py:316
  24.0 5.9 %collective-permute-start.9 = (bf16[528,256]{1,0:T(8,128)(2,1)S(1)}, bf16[528,256]{1,0:T(8,128)(2,1)S(1)}, u32[]{:S(2)}, u32[]{:S(2)}) collective-permute-start(bf16[528,256]{1,0:T(8,128)(2,1)S(1)} %collective-permute-done.7.xs), channel_id=1, source_target_pairs={{0,1},{1,0},{2,3},{3,2},{4,5},{5,4},{6,7},{7,6},{8,9},{9,8},{10,11... | collective-permute-start | bytes 811016 | tf_op jit(solution)/shard_map/ppermute | solution.py:284
  30.0 1.5 %collective-permute-start.8 = (bf16[528,256]{1,0:T(8,128)(2,1)S(1)}, bf16[528,256]{1,0:T(8,128)(2,1)S(1)}, u32[]{:S(2)}, u32[]{:S(2)}) collective-permute-start(bf16[528,256]{1,0:T(8,128)(2,1)S(1)} %collective-permute-done.4.far1), channel_id=1, source_target_pairs={{0,1},{1,0},{2,3},{3,2},{4,5},{5,4},{6,7},{7,6},{8,9},{9,8},{10,11... | collective-permute-start | bytes 811016 | tf_op jit(solution)/shard_map/ppermute | solution.py:284

commit v4 on v3

--- a/solution.py
+++ b/solution.py
@@ -306,19 +306,6 @@
         cost_estimate=cost(4),
     )(spatial_first, spatial_second, disparity_weight.T)
 
-    par0, w1 = lax.optimization_barrier((par0, w1))
-    if bands % 2:
-        onward.append((bands - 1, bands - 2))
-
-    def send_on(chunk, x):
-        if bands % 2:
-            x = jnp.where(row == bands - 1, chunk, x)
-        return lax.ppermute(x, "rows", onward)
-
-    far0 = send_on(chunks[0], par0)
-    par0_n = cross(par0)
-
-    par0, own_n[0] = lax.optimization_barrier((par0, own_n[0]))
     o0, o1 = pl.pallas_call(
         own_kernel,
         out_shape=[volume_out] * 2,
@@ -328,8 +315,18 @@
         compiler_params=LIMIT,
         cost_estimate=cost(4),
     )(*chunks, *own_n)
-    far0, o0 = lax.optimization_barrier((far0, o0))
-    par1, o1 = lax.optimization_barrier((par1, o1))
+    par0, w1, o0 = lax.optimization_barrier((par0, w1, o0))
+    if bands % 2:
+        onward.append((bands - 1, bands - 2))
+
+    def send_on(chunk, x):
+        if bands % 2:
+            x = jnp.where(row == bands - 1, chunk, x)
+        return lax.ppermute(x, "rows", onward)
+
+    far0 = send_on(chunks[0], par0)
+    par0_n = cross(par0)
+
     far1 = send_on(chunks[1], par1)
     par1_n = cross(par1)
     par1_n, far0 = lax.optimization_barrier((par1_n, far0))

time: 40.3 us -> 39.3 us (0.975)
  waiting for transfers between devices: 6.28 us -> 5.34 us
    ppermute x2, waiting for transfers between devices: 5.5 us -> 4.67 us  [body(): par0, par1 = [lax.ppermute(x, 'rows', partners) for x in chunks]]
  transfers between devices with their start and end apart: 10 -> 10, of which waited for: 3 -> 4; matrix products, arithmetic and copies ran while one was open for 0% -> 0% of each run, Pallas kernels for 26% -> 27%
where the time goes in v4:
time: 39.3 us; the launch traced here: 39.1 us
  Pallas kernels  21.8 us (55%)
  starting transfers between devices  11.8 us (30%)
  waiting for transfers between devices  5.34 us (14%)
    pallas_call x1, Pallas kernels, body(): pl.pallas_call(last_kernel, out_shape=jax.ShapeDtypeStruct((row_count, co...  8.5 us
    ppermute x2, starting transfers between devices, send_on(): return lax.ppermute(x, 'rows', onward)  7.64 us
    pallas_call x1, Pallas kernels, body(): pl.pallas_call(partner_kernel, out_shape=jax.ShapeDtypeStruct(pair, BF),...  5.22 us
    ppermute x2, waiting for transfers between devices, body(): par0, par1 = [lax.ppermute(x, 'rows', partners) for x in chunks]  4.67 us
    ppermute x2, starting transfers between devices, body(): par0, par1 = [lax.ppermute(x, 'rows', partners) for x in chunks]  2.86 us
    pallas_call x1, Pallas kernels, body(): pl.pallas_call(pack_kernel, out_shape=[packed, packed], in_specs=[HBM, HB...  2.73 us
    pallas_call x1, Pallas kernels, body(): pl.pallas_call(own_kernel, out_shape=[volume_out] * 2, in_specs=[VMEM] *...  2.57 us
    pallas_call x1, Pallas kernels, body(): pl.pallas_call(weights_kernel, out_shape=[jax.ShapeDtypeStruct((2, STEP1...  1.41 us
  transfers between devices with their start and end apart: 10, of which 4 were waited for; matrix products, arithmetic and copies ran while one was open for 0% of the time, Pallas kernels for 27%

profile of v4, /device:TPU:0, one launch (start us, length us, event | category | flops | bytes accessed | tf_op | source)
XLA Modules:
  0.0 39.1 jit_solution(15184414750781446182)
XLA Ops:
  0.0 0.0 copy-start.4
  0.0 0.0 copy-start.2
  0.0 0.0 copy-start.3
  0.0 2.7 %shard_map.73 = (bf16[528,256]{1,0:T(8,128)(2,1)}, bf16[528,256]{1,0:T(8,128)(2,1)}) custom-call(bf16[2,256,256]{2,1,0:T(8,128)(2,1)} %left.1, bf16[2,256,256]{2,1,0:T(8,128)(2,1)} %right.1, s32[1,2,4]{2,1,0:T(2,128)} %bitcast.3, s32[1,4]{1,0:T(1,128)} %block_count.1), custom_call_target="tpu_custom_call" | custom-call | flops 1000000000 | bytes 1000000 | tf_op jit(solution)/shard_map/pallas_call | solution.py:269
  2.7 0.5 %collective-permute-start.3 = (bf16[528,256]{1,0:T(8,128)(2,1)}, bf16[528,256]{1,0:T(8,128)(2,1)S(1)}, u32[]{:S(2)}, u32[]{:S(2)}) collective-permute-start(bf16[528,256]{1,0:T(8,128)(2,1)} %get-tuple-element.20.own0), channel_id=1, source_target_pairs={{0,1},{1,0},{2,3},{3,2},{4,5},{5,4},{6,7},{7,6},{8,9},{9,8},{10,11... | collective-permute-start | bytes 811016 | tf_op jit(solution)/shard_map/ppermute | solution.py:284
  3.3 2.6 %collective-permute-start.2 = (bf16[528,256]{1,0:T(8,128)(2,1)}, bf16[528,256]{1,0:T(8,128)(2,1)S(1)}, u32[]{:S(2)}, u32[]{:S(2)}) collective-permute-start(bf16[528,256]{1,0:T(8,128)(2,1)} %get-tuple-element.20.own0), channel_id=1, source_target_pairs={{0,2},{2,0},{4,6},{6,4},{8,10},{10,8},{12,14},{14,12},{1,3},{3,1},... | collective-permute-start | bytes 811016 | tf_op jit(solution)/shard_map/ppermute | solution.py:286
  5.9 0.2 collective-permute-start.4
  6.0 0.3 collective-permute-start
  6.3 0.0 copy-done.4
  6.3 0.0 copy-done.2
  6.3 0.0 copy-done.3
  6.3 0.0 copy-start
  6.3 0.0 copy-start.1
  6.3 1.4 %shard_map.74 = (bf16[2,192,256]{2,1,0:T(8,128)(2,1)S(1)}, bf16[3,128,480]{2,1,0:T(8,128)(2,1)S(1)}, bf16[4096,256]{1,0:T(8,128)(2,1)S(1)}) custom-call(bf16[3,3,16,16]{3,2,1,0:T(8,128)(2,1)S(1)} %copy-done.2, bf16[3,3,16,16]{3,2,1,0:T(8,128)(2,1)S(1)} %copy-done.3, bf16[16,17]{1,0:T(8,128)(2,1)S(1)} %bitcast.2), custom_call_target="tpu_custom_call" | custom-call | flops 4000000000 | bytes 4000000 | tf_op jit(solution)/shard_map/pallas_call | solution.py:296
  7.7 0.0 collective-permute-done.3.own0_n
  7.7 0.0 collective-permute-done.4.own1_n
  7.8 0.0 copy-done
  7.8 0.0 copy-done.1
  7.8 2.6 %shard_map.75 = (bf16[260,16,256]{2,1,0:T(8,128)(2,1)S(1)}, bf16[260,16,256]{2,1,0:T(8,128)(2,1)S(1)}) custom-call(bf16[528,256]{1,0:T(8,128)(2,1)S(1)} %copy-done.1, bf16[528,256]{1,0:T(8,128)(2,1)S(1)} %copy-done, bf16[528,256]{1,0:T(8,128)(2,1)S(1)} %collective-permute-done.3.own0_n, bf16[528,256]{1,0:T(8,128)(2,1)S(1)} %collective-permute-done.4.own1_n), custom_call_target="tpu_custom_call" | custom-call | flops 4000000000 | bytes 4000000 | tf_op jit(solution)/shard_map/pallas_call | solution.py:309
  10.4 3.1 %collective-permute-done.2.par0 = bf16[528,256]{1,0:T(8,128)(2,1)S(1)} collective-permute-done((bf16[528,256]{1,0:T(8,128)(2,1)}, bf16[528,256]{1,0:T(8,128)(2,1)S(1)}, u32[]{:S(2)}, u32[]{:S(2)}) %collective-permute-start.2) | collective-permute-done | bytes 270368 | tf_op jit(solution)/shard_map/ppermute | solution.py:286
  13.4 3.9 %collective-permute-start.7 = (bf16[528,256]{1,0:T(8,128)(2,1)S(1)}, bf16[528,256]{1,0:T(8,128)(2,1)S(1)}, u32[]{:S(2)}, u32[]{:S(2)}) collective-permute-start(bf16[528,256]{1,0:T(8,128)(2,1)S(1)} %collective-permute-done.2.par0), channel_id=1, source_target_pairs={{0,4},{4,8},{6,2},{8,12},{10,6},{14,10},{1,5},{5,9},{7,3},{9,13},{... | collective-permute-start | bytes 811016 | tf_op jit(solution)/shard_map/ppermute | solution.py:325
  17.3 1.6 %collective-permute-done.par1 = bf16[528,256]{1,0:T(8,128)(2,1)S(1)} collective-permute-done((bf16[528,256]{1,0:T(8,128)(2,1)}, bf16[528,256]{1,0:T(8,128)(2,1)S(1)}, u32[]{:S(2)}, u32[]{:S(2)}) %collective-permute-start) | collective-permute-done | bytes 270368 | tf_op jit(solution)/shard_map/ppermute | solution.py:286
  18.9 0.0 collective-permute-start.6
  18.9 0.5 %collective-permute-start.5 = (bf16[528,256]{1,0:T(8,128)(2,1)S(1)}, bf16[528,256]{1,0:T(8,128)(2,1)S(1)}, u32[]{:S(2)}, u32[]{:S(2)}) collective-permute-start(bf16[528,256]{1,0:T(8,128)(2,1)S(1)} %collective-permute-done.2.par0), channel_id=1, source_target_pairs={{0,1},{1,0},{2,3},{3,2},{4,5},{5,4},{6,7},{7,6},{8,9},{9,8},{10,11... | collective-permute-start | bytes 811016 | tf_op jit(solution)/shard_map/ppermute | solution.py:284
  19.5 3.7 %collective-permute-start.1 = (bf16[528,256]{1,0:T(8,128)(2,1)S(1)}, bf16[528,256]{1,0:T(8,128)(2,1)S(1)}, u32[]{:S(2)}, u32[]{:S(2)}) collective-permute-start(bf16[528,256]{1,0:T(8,128)(2,1)S(1)} %collective-permute-done.par1), channel_id=1, source_target_pairs={{0,4},{4,8},{6,2},{8,12},{10,6},{14,10},{1,5},{5,9},{7,3},{9,13},{... | collective-permute-start | bytes 811016 | tf_op jit(solution)/shard_map/ppermute | solution.py:325
  23.2 0.0 collective-permute-done.7.xs
  23.2 0.0 collective-permute-done.6.par1_n
  23.2 0.1 collective-permute-start.9
  23.3 0.0 collective-permute-done.5.par0_n
  23.3 5.2 %shard_map.76.partner = bf16[258,32,256]{2,1,0:T(8,128)(2,1)S(1)} custom-call(bf16[528,256]{1,0:T(8,128)(2,1)S(1)} %collective-permute-done.2.par0, bf16[528,256]{1,0:T(8,128)(2,1)S(1)} %collective-permute-done.par1, bf16[528,256]{1,0:T(8,128)(2,1)S(1)} %collective-permute-done.5.par0_n, bf16[528,256]{1,0:T(8,128)(2,1)S(1)} %collective-permute-done.6.par1_n, ...), custom_call_target="tpu_custom_call" | custom-call | flops 8000000000 | bytes 8000000 | tf_op jit(solution)/shard_map/pallas_call | solution.py:334
  28.5 0.5 %collective-permute-done.1.far1 = bf16[528,256]{1,0:T(8,128)(2,1)S(1)} collective-permute-done((bf16[528,256]{1,0:T(8,128)(2,1)S(1)}, bf16[528,256]{1,0:T(8,128)(2,1)S(1)}, u32[]{:S(2)}, u32[]{:S(2)}) %collective-permute-start.1) | collective-permute-done | bytes 270368 | tf_op jit(solution)/shard_map/ppermute | solution.py:325
  29.1 0.0 collective-permute-start.8
  29.1 0.0 collective-permute-done.9.xn
  29.1 1.4 %shard_map.77.f0 = bf16[260,16,256]{2,1,0:T(8,128)(2,1)S(1)} custom-call(bf16[528,256]{1,0:T(8,128)(2,1)S(1)} %collective-permute-done.7.xs, bf16[528,256]{1,0:T(8,128)(2,1)S(1)} %collective-permute-done.9.xn), custom_call_target="tpu_custom_call" | custom-call | flops 1000000000 | bytes 1000000 | tf_op jit(solution)/shard_map/pallas_call | solution.py:345
  30.5 0.1 collective-permute-done.8.far1_n
  30.6 8.5 %shard_map.78 = f32[2,256,256]{2,1,0:T(8,128)} custom-call(bf16[528,256]{1,0:T(8,128)(2,1)S(1)} %collective-permute-done.1.far1, bf16[528,256]{1,0:T(8,128)(2,1)S(1)} %collective-permute-done.8.far1_n, bf16[260,16,256]{2,1,0:T(8,128)(2,1)S(1)} %shard_map.77.f0, bf16[260,16,256]{2,1,0:T(8,128)(2,1)S(1)} %get-tuple-element.25.o0, ...), custom_call_target="tpu_custom_call" | custom-call | flops 12000000000 | bytes 12000000 | tf_op jit(solution)/shard_map/pallas_call | solution.py:355
Async XLA Ops:
  0.0 6.3 %copy-start.4 = (bf16[17,16]{0,1:T(8,128)(2,1)S(1)}, bf16[17,16]{0,1:T(8,128)(2,1)}, u32[]{:S(2)}) copy-start(bf16[17,16]{0,1:T(8,128)(2,1)} %param.13) | copy-start | bytes 1636
  0.0 6.3 %copy-start.2 = (bf16[3,3,16,16]{3,2,1,0:T(8,128)(2,1)S(1)}, bf16[3,3,16,16]{3,2,1,0:T(8,128)(2,1)}, u32[]{:S(2)}) copy-start(bf16[3,3,16,16]{3,2,1,0:T(8,128)(2,1)} %s1_.1) | copy-start | bytes 13828
  0.0 6.3 %copy-start.3 = (bf16[3,3,16,16]{3,2,1,0:T(8,128)(2,1)S(1)}, bf16[3,3,16,16]{3,2,1,0:T(8,128)(2,1)}, u32[]{:S(2)}) copy-start(bf16[3,3,16,16]{3,2,1,0:T(8,128)(2,1)} %s2_.1) | copy-start | bytes 13828
  2.7 5.0 %collective-permute-start.3 = (bf16[528,256]{1,0:T(8,128)(2,1)}, bf16[528,256]{1,0:T(8,128)(2,1)S(1)}, u32[]{:S(2)}, u32[]{:S(2)}) collective-permute-start(bf16[528,256]{1,0:T(8,128)(2,1)} %get-tuple-element.20.own0), channel_id=1, source_target_pairs={{0,1},{1,0},{2,3},{3,2},{4,5},{5,4},{6,7},{7,6},{8,9},{9,8},{10,11... | collective-permute-start | bytes 811016 | tf_op jit(solution)/shard_map/ppermute | solution.py:284
  3.3 10.1 %collective-permute-start.2 = (bf16[528,256]{1,0:T(8,128)(2,1)}, bf16[528,256]{1,0:T(8,128)(2,1)S(1)}, u32[]{:S(2)}, u32[]{:S(2)}) collective-permute-start(bf16[528,256]{1,0:T(8,128)(2,1)} %get-tuple-element.20.own0), channel_id=1, source_target_pairs={{0,2},{2,0},{4,6},{6,4},{8,10},{10,8},{12,14},{14,12},{1,3},{3,1},... | collective-permute-start | bytes 811016 | tf_op jit(solution)/shard_map/ppermute | solution.py:286
  5.9 1.9 %collective-permute-start.4 = (bf16[528,256]{1,0:T(8,128)(2,1)}, bf16[528,256]{1,0:T(8,128)(2,1)S(1)}, u32[]{:S(2)}, u32[]{:S(2)}) collective-permute-start(bf16[528,256]{1,0:T(8,128)(2,1)} %get-tuple-element.19.own1), channel_id=1, source_target_pairs={{0,1},{1,0},{2,3},{3,2},{4,5},{5,4},{6,7},{7,6},{8,9},{9,8},{10,11... | collective-permute-start | bytes 811016 | tf_op jit(solution)/shard_map/ppermute | solution.py:284
  6.0 12.9 %collective-permute-start = (bf16[528,256]{1,0:T(8,128)(2,1)}, bf16[528,256]{1,0:T(8,128)(2,1)S(1)}, u32[]{:S(2)}, u32[]{:S(2)}) collective-permute-start(bf16[528,256]{1,0:T(8,128)(2,1)} %get-tuple-element.19.own1), channel_id=1, source_target_pairs={{0,2},{2,0},{4,6},{6,4},{8,10},{10,8},{12,14},{14,12},{1,3},{3,1},... | collective-permute-start | bytes 811016 | tf_op jit(solution)/shard_map/ppermute | solution.py:286
  6.3 1.5 %copy-start = (bf16[528,256]{1,0:T(8,128)(2,1)S(1)}, bf16[528,256]{1,0:T(8,128)(2,1)}, u32[]{:S(2)}) copy-start(bf16[528,256]{1,0:T(8,128)(2,1)} %get-tuple-element.19.own1) | copy-start | bytes 811012
  6.3 1.5 %copy-start.1 = (bf16[528,256]{1,0:T(8,128)(2,1)S(1)}, bf16[528,256]{1,0:T(8,128)(2,1)}, u32[]{:S(2)}) copy-start(bf16[528,256]{1,0:T(8,128)(2,1)} %get-tuple-element.20.own0) | copy-start | bytes 811012
  13.4 9.8 %collective-permute-start.7 = (bf16[528,256]{1,0:T(8,128)(2,1)S(1)}, bf16[528,256]{1,0:T(8,128)(2,1)S(1)}, u32[]{:S(2)}, u32[]{:S(2)}) collective-permute-start(bf16[528,256]{1,0:T(8,128)(2,1)S(1)} %collective-permute-done.2.par0), channel_id=1, source_target_pairs={{0,4},{4,8},{6,2},{8,12},{10,6},{14,10},{1,5},{5,9},{7,3},{9,13},{... | collective-permute-start | bytes 811016 | tf_op jit(solution)/shard_map/ppermute | solution.py:325
  18.9 4.3 %collective-permute-start.6 = (bf16[528,256]{1,0:T(8,128)(2,1)S(1)}, bf16[528,256]{1,0:T(8,128)(2,1)S(1)}, u32[]{:S(2)}, u32[]{:S(2)}) collective-permute-start(bf16[528,256]{1,0:T(8,128)(2,1)S(1)} %collective-permute-done.par1), channel_id=1, source_target_pairs={{0,1},{1,0},{2,3},{3,2},{4,5},{5,4},{6,7},{7,6},{8,9},{9,8},{10,11... | collective-permute-start | bytes 811016 | tf_op jit(solution)/shard_map/ppermute | solution.py:284
  18.9 4.3 %collective-permute-start.5 = (bf16[528,256]{1,0:T(8,128)(2,1)S(1)}, bf16[528,256]{1,0:T(8,128)(2,1)S(1)}, u32[]{:S(2)}, u32[]{:S(2)}) collective-permute-start(bf16[528,256]{1,0:T(8,128)(2,1)S(1)} %collective-permute-done.2.par0), channel_id=1, source_target_pairs={{0,1},{1,0},{2,3},{3,2},{4,5},{5,4},{6,7},{7,6},{8,9},{9,8},{10,11... | collective-permute-start | bytes 811016 | tf_op jit(solution)/shard_map/ppermute | solution.py:284
  19.5 9.6 %collective-permute-start.1 = (bf16[528,256]{1,0:T(8,128)(2,1)S(1)}, bf16[528,256]{1,0:T(8,128)(2,1)S(1)}, u32[]{:S(2)}, u32[]{:S(2)}) collective-permute-start(bf16[528,256]{1,0:T(8,128)(2,1)S(1)} %collective-permute-done.par1), channel_id=1, source_target_pairs={{0,4},{4,8},{6,2},{8,12},{10,6},{14,10},{1,5},{5,9},{7,3},{9,13},{... | collective-permute-start | bytes 811016 | tf_op jit(solution)/shard_map/ppermute | solution.py:325
  23.2 5.9 %collective-permute-start.9 = (bf16[528,256]{1,0:T(8,128)(2,1)S(1)}, bf16[528,256]{1,0:T(8,128)(2,1)S(1)}, u32[]{:S(2)}, u32[]{:S(2)}) collective-permute-start(bf16[528,256]{1,0:T(8,128)(2,1)S(1)} %collective-permute-done.7.xs), channel_id=1, source_target_pairs={{0,1},{1,0},{2,3},{3,2},{4,5},{5,4},{6,7},{7,6},{8,9},{9,8},{10,11... | collective-permute-start | bytes 811016 | tf_op jit(solution)/shard_map/ppermute | solution.py:284
  29.1 1.5 %collective-permute-start.8 = (bf16[528,256]{1,0:T(8,128)(2,1)S(1)}, bf16[528,256]{1,0:T(8,128)(2,1)S(1)}, u32[]{:S(2)}, u32[]{:S(2)}) collective-permute-start(bf16[528,256]{1,0:T(8,128)(2,1)S(1)} %collective-permute-done.1.far1), channel_id=1, source_target_pairs={{0,1},{1,0},{2,3},{3,2},{4,5},{5,4},{6,7},{7,6},{8,9},{9,8},{10,11... | collective-permute-start | bytes 811016 | tf_op jit(solution)/shard_map/ppermute | solution.py:284

commit v5 on v4

--- a/solution.py
+++ b/solution.py
@@ -1,3 +1,5 @@
+import functools
+
 import jax
 import jax.numpy as jnp
 from jax import lax
@@ -36,15 +38,14 @@
     return col == 0, col == cols - 1, row == 0, row == rows - 1, row % 2
 
 
-def pack_kernel(left, right, block_list, block_count, p0, p1, sems):
+def pack_kernel(c, left, right, block_list, block_count, pack, sems):
     cols = left.shape[1]
     copies = []
-    for c, p in enumerate((p0, p1)):
-        for i, src in enumerate((left, right)):
-            dst = p.at[pl.ds(i * cols, cols), :]
-            copies.append(pltpu.make_async_copy(src.at[c], dst, sems.at[2 * c + i]))
-            copies[-1].start()
-    ndisp = p0.shape[1]
+    for i, src in enumerate((left, right)):
+        dst = pack.at[pl.ds(i * cols, cols), :]
+        copies.append(pltpu.make_async_copy(src.at[c], dst, sems.at[i]))
+        copies[-1].start()
+    ndisp = pack.shape[1]
     lane_block = (ndisp - 1 - iota((TILE // 16, ndisp), 1)) // DB
     lines = []
     for tile in range(cols // TILE):
@@ -53,9 +54,7 @@
             listed = jnp.where(slot < block_count[0, tile], block_list[0, slot, tile], -1)
             line = jnp.where(lane_block == listed, 1.0, line)
         lines.append(line)
-    lines = jnp.concatenate(lines, axis=0).astype(BF)
-    for p in (p0, p1):
-        p[2 * cols :, :] = lines
+    pack[2 * cols :, :] = jnp.concatenate(lines, axis=0).astype(BF)
     for copy in copies:
         copy.wait()
 
@@ -266,14 +265,18 @@
     bands = lax.axis_size("rows")
     row = lax.axis_index("rows")
     packed = jax.ShapeDtypeStruct((2 * cols + 16, channels), BF)
-    chunks = pl.pallas_call(
-        pack_kernel,
-        out_shape=[packed, packed],
-        in_specs=[HBM, HBM, SMEM, SMEM],
-        out_specs=[VMEM, VMEM],
-        scratch_shapes=[pltpu.SemaphoreType.DMA((4,))],
-        cost_estimate=cost(1),
-    )(left_feat, right_feat, block_list.transpose(0, 2, 1), block_count)
+    lists = block_list.transpose(0, 2, 1)
+    chunks = [
+        pl.pallas_call(
+            functools.partial(pack_kernel, c),
+            out_shape=packed,
+            in_specs=[HBM, HBM, SMEM, SMEM],
+            out_specs=VMEM,
+            scratch_shapes=[pltpu.SemaphoreType.DMA((2,))],
+            cost_estimate=cost(1),
+        )(left_feat, right_feat, lists, block_count)
+        for c in range(row_count)
+    ]
 
     partners = [(i, i ^ 1) for i in range(bands) if i ^ 1 < bands]
     onward = [(i, i + 2 - 4 * (i % 2)) for i in range(bands)]

time: 39.3 us -> 39.3 us (level)
  waiting for transfers between devices: 5.34 us -> 2.59 us
  Pallas kernels: 21.8 us -> 24.2 us
    ppermute x2, waiting for transfers between devices: 4.67 us -> 2.22 us  [body(): par0, par1 = [lax.ppermute(x, 'rows', partners) for x in chunks]]
    pallas_call x1 -> x2, Pallas kernels: 2.73 us -> 4.74 us  [body(): pl.pallas_call(functools.partial(pack_kernel, c), out_shape=packed, in_sp...]
  transfers between devices with their start and end apart: 10 -> 10, of which waited for: 4 -> 3; matrix products, arithmetic and copies ran while one was open for 0% -> 0% of each run, Pallas kernels for 27% -> 34%
where the time goes in v5:
time: 39.3 us; the launch traced here: 39.1 us
  Pallas kernels  24.2 us (62%)
  starting transfers between devices  12.1 us (31%)
  waiting for transfers between devices  2.59 us (7%)
    pallas_call x1, Pallas kernels, body(): pl.pallas_call(last_kernel, out_shape=jax.ShapeDtypeStruct((row_count, co...  8.7 us
    ppermute x2, starting transfers between devices, send_on(): return lax.ppermute(x, 'rows', onward)  7.64 us
    pallas_call x1, Pallas kernels, body(): pl.pallas_call(partner_kernel, out_shape=jax.ShapeDtypeStruct(pair, BF),...  5.41 us
    pallas_call x2, Pallas kernels, body(): pl.pallas_call(functools.partial(pack_kernel, c), out_shape=packed, in_sp...  4.74 us
    ppermute x2, starting transfers between devices, body(): par0, par1 = [lax.ppermute(x, 'rows', partners) for x in chunks]  2.86 us
    pallas_call x1, Pallas kernels, body(): pl.pallas_call(own_kernel, out_shape=[volume_out] * 2, in_specs=[VMEM] *...  2.57 us
    ppermute x2, waiting for transfers between devices, body(): par0, par1 = [lax.ppermute(x, 'rows', partners) for x in chunks]  2.22 us
    ppermute x6, starting transfers between devices, cross(): return lax.ppermute(x, 'cols', across)  1.56 us
  transfers between devices with their start and end apart: 10, of which 3 were waited for; matrix products, arithmetic and copies ran while one was open for 0% of the time, Pallas kernels for 34%

profile of v5, /device:TPU:0, one launch (start us, length us, event | category | flops | bytes accessed | tf_op | source)
XLA Modules:
  0.0 39.1 jit_solution(8969161989411301353)
XLA Ops:
  0.0 2.4 %shard_map.74.own0 = bf16[528,256]{1,0:T(8,128)(2,1)} custom-call(bf16[2,256,256]{2,1,0:T(8,128)(2,1)} %left.3, bf16[2,256,256]{2,1,0:T(8,128)(2,1)} %right.3, s32[1,2,4]{2,1,0:T(2,128)} %bitcast.3, s32[1,4]{1,0:T(1,128)} %block_count.3), custom_call_target="tpu_custom_call" | custom-call | flops 1000000000 | bytes 1000000 | tf_op jit(solution)/shard_map/pallas_call | solution.py:270
  2.4 0.0 copy-start.2
  2.4 0.0 copy-start.3
  2.4 0.0 copy-start.4
  2.4 0.5 %collective-permute-start.3 = (bf16[528,256]{1,0:T(8,128)(2,1)}, bf16[528,256]{1,0:T(8,128)(2,1)S(1)}, u32[]{:S(2)}, u32[]{:S(2)}) collective-permute-start(bf16[528,256]{1,0:T(8,128)(2,1)} %shard_map.74.own0), channel_id=1, source_target_pairs={{0,1},{1,0},{2,3},{3,2},{4,5},{5,4},{6,7},{7,6},{8,9},{9,8},{10,11... | collective-permute-start | bytes 811016 | tf_op jit(solution)/shard_map/ppermute | solution.py:287
  2.9 2.6 %collective-permute-start.2 = (bf16[528,256]{1,0:T(8,128)(2,1)}, bf16[528,256]{1,0:T(8,128)(2,1)S(1)}, u32[]{:S(2)}, u32[]{:S(2)}) collective-permute-start(bf16[528,256]{1,0:T(8,128)(2,1)} %shard_map.74.own0), channel_id=1, source_target_pairs={{0,2},{2,0},{4,6},{6,4},{8,10},{10,8},{12,14},{14,12},{1,3},{3,1},... | collective-permute-start | bytes 811016 | tf_op jit(solution)/shard_map/ppermute | solution.py:289
  5.5 2.4 %shard_map.73.own1 = bf16[528,256]{1,0:T(8,128)(2,1)} custom-call(bf16[2,256,256]{2,1,0:T(8,128)(2,1)} %left.3, bf16[2,256,256]{2,1,0:T(8,128)(2,1)} %right.3, s32[1,2,4]{2,1,0:T(2,128)} %bitcast.4, s32[1,4]{1,0:T(1,128)} %block_count.3), custom_call_target="tpu_custom_call" | custom-call | flops 1000000000 | bytes 1000000 | tf_op jit(solution)/shard_map/pallas_call | solution.py:270
  7.9 0.2 collective-permute-start.4
  8.1 0.3 collective-permute-start
  8.4 0.0 copy-done.2
  8.4 0.0 copy-done.3
  8.4 0.0 copy-done.4
  8.4 0.0 copy-start
  8.4 0.0 copy-start.1
  8.4 1.4 %shard_map.75 = (bf16[2,192,256]{2,1,0:T(8,128)(2,1)S(1)}, bf16[3,128,480]{2,1,0:T(8,128)(2,1)S(1)}, bf16[4096,256]{1,0:T(8,128)(2,1)S(1)}) custom-call(bf16[3,3,16,16]{3,2,1,0:T(8,128)(2,1)S(1)} %copy-done.2, bf16[3,3,16,16]{3,2,1,0:T(8,128)(2,1)S(1)} %copy-done.3, bf16[16,17]{1,0:T(8,128)(2,1)S(1)} %bitcast.2), custom_call_target="tpu_custom_call" | custom-call | flops 4000000000 | bytes 4000000 | tf_op jit(solution)/shard_map/pallas_call | solution.py:299
  9.8 0.0 collective-permute-done.3.own0_n
  9.8 0.0 collective-permute-done.4.own1_n
  9.9 0.0 copy-done
  9.9 0.0 copy-done.1
  9.9 2.6 %shard_map.76 = (bf16[260,16,256]{2,1,0:T(8,128)(2,1)S(1)}, bf16[260,16,256]{2,1,0:T(8,128)(2,1)S(1)}) custom-call(bf16[528,256]{1,0:T(8,128)(2,1)S(1)} %copy-done, bf16[528,256]{1,0:T(8,128)(2,1)S(1)} %copy-done.1, bf16[528,256]{1,0:T(8,128)(2,1)S(1)} %collective-permute-done.3.own0_n, bf16[528,256]{1,0:T(8,128)(2,1)S(1)} %collective-permute-done.4.own1_n), custom_call_target="tpu_custom_call" | custom-call | flops 4000000000 | bytes 4000000 | tf_op jit(solution)/shard_map/pallas_call | solution.py:312
  12.5 0.6 %collective-permute-done.2.par0 = bf16[528,256]{1,0:T(8,128)(2,1)S(1)} collective-permute-done((bf16[528,256]{1,0:T(8,128)(2,1)}, bf16[528,256]{1,0:T(8,128)(2,1)S(1)}, u32[]{:S(2)}, u32[]{:S(2)}) %collective-permute-start.2) | collective-permute-done | bytes 270368 | tf_op jit(solution)/shard_map/ppermute | solution.py:289
  13.1 3.9 %collective-permute-start.7 = (bf16[528,256]{1,0:T(8,128)(2,1)S(1)}, bf16[528,256]{1,0:T(8,128)(2,1)S(1)}, u32[]{:S(2)}, u32[]{:S(2)}) collective-permute-start(bf16[528,256]{1,0:T(8,128)(2,1)S(1)} %collective-permute-done.2.par0), channel_id=1, source_target_pairs={{0,4},{4,8},{6,2},{8,12},{10,6},{14,10},{1,5},{5,9},{7,3},{9,13},{... | collective-permute-start | bytes 811016 | tf_op jit(solution)/shard_map/ppermute | solution.py:328
  17.0 1.6 %collective-permute-done.par1 = bf16[528,256]{1,0:T(8,128)(2,1)S(1)} collective-permute-done((bf16[528,256]{1,0:T(8,128)(2,1)}, bf16[528,256]{1,0:T(8,128)(2,1)S(1)}, u32[]{:S(2)}, u32[]{:S(2)}) %collective-permute-start) | collective-permute-done | bytes 270368 | tf_op jit(solution)/shard_map/ppermute | solution.py:289
  18.6 0.0 collective-permute-start.6
  18.6 0.5 %collective-permute-start.5 = (bf16[528,256]{1,0:T(8,128)(2,1)S(1)}, bf16[528,256]{1,0:T(8,128)(2,1)S(1)}, u32[]{:S(2)}, u32[]{:S(2)}) collective-permute-start(bf16[528,256]{1,0:T(8,128)(2,1)S(1)} %collective-permute-done.2.par0), channel_id=1, source_target_pairs={{0,1},{1,0},{2,3},{3,2},{4,5},{5,4},{6,7},{7,6},{8,9},{9,8},{10,11... | collective-permute-start | bytes 811016 | tf_op jit(solution)/shard_map/ppermute | solution.py:287
  19.1 3.7 %collective-permute-start.1 = (bf16[528,256]{1,0:T(8,128)(2,1)S(1)}, bf16[528,256]{1,0:T(8,128)(2,1)S(1)}, u32[]{:S(2)}, u32[]{:S(2)}) collective-permute-start(bf16[528,256]{1,0:T(8,128)(2,1)S(1)} %collective-permute-done.par1), channel_id=1, source_target_pairs={{0,4},{4,8},{6,2},{8,12},{10,6},{14,10},{1,5},{5,9},{7,3},{9,13},{... | collective-permute-start | bytes 811016 | tf_op jit(solution)/shard_map/ppermute | solution.py:328
  22.8 0.0 collective-permute-done.7.xs
  22.9 0.0 collective-permute-done.6.par1_n
  22.9 0.1 collective-permute-start.9
  22.9 0.0 collective-permute-done.5.par0_n
  23.0 5.4 %shard_map.77.partner = bf16[258,32,256]{2,1,0:T(8,128)(2,1)S(1)} custom-call(bf16[528,256]{1,0:T(8,128)(2,1)S(1)} %collective-permute-done.2.par0, bf16[528,256]{1,0:T(8,128)(2,1)S(1)} %collective-permute-done.par1, bf16[528,256]{1,0:T(8,128)(2,1)S(1)} %collective-permute-done.5.par0_n, bf16[528,256]{1,0:T(8,128)(2,1)S(1)} %collective-permute-done.6.par1_n, ...), custom_call_target="tpu_custom_call" | custom-call | flops 8000000000 | bytes 8000000 | tf_op jit(solution)/shard_map/pallas_call | solution.py:337
  28.4 0.3 collective-permute-done.1.far1
  28.7 0.2 collective-permute-start.8
  29.0 0.0 collective-permute-done.9.xn
  29.0 1.4 %shard_map.78.f0 = bf16[260,16,256]{2,1,0:T(8,128)(2,1)S(1)} custom-call(bf16[528,256]{1,0:T(8,128)(2,1)S(1)} %collective-permute-done.7.xs, bf16[528,256]{1,0:T(8,128)(2,1)S(1)} %collective-permute-done.9.xn), custom_call_target="tpu_custom_call" | custom-call | flops 1000000000 | bytes 1000000 | tf_op jit(solution)/shard_map/pallas_call | solution.py:348
  30.3 0.0 collective-permute-done.8.far1_n
  30.4 8.7 %shard_map.79 = f32[2,256,256]{2,1,0:T(8,128)} custom-call(bf16[528,256]{1,0:T(8,128)(2,1)S(1)} %collective-permute-done.1.far1, bf16[528,256]{1,0:T(8,128)(2,1)S(1)} %collective-permute-done.8.far1_n, bf16[260,16,256]{2,1,0:T(8,128)(2,1)S(1)} %shard_map.78.f0, bf16[260,16,256]{2,1,0:T(8,128)(2,1)S(1)} %get-tuple-element.21.o0, ...), custom_call_target="tpu_custom_call" | custom-call | flops 12000000000 | bytes 12000000 | tf_op jit(solution)/shard_map/pallas_call | solution.py:358
Async XLA Ops:
  2.4 6.0 %copy-start.2 = (bf16[3,3,16,16]{3,2,1,0:T(8,128)(2,1)S(1)}, bf16[3,3,16,16]{3,2,1,0:T(8,128)(2,1)}, u32[]{:S(2)}) copy-start(bf16[3,3,16,16]{3,2,1,0:T(8,128)(2,1)} %s1_.1) | copy-start | bytes 13828
  2.4 6.0 %copy-start.3 = (bf16[3,3,16,16]{3,2,1,0:T(8,128)(2,1)S(1)}, bf16[3,3,16,16]{3,2,1,0:T(8,128)(2,1)}, u32[]{:S(2)}) copy-start(bf16[3,3,16,16]{3,2,1,0:T(8,128)(2,1)} %s2_.1) | copy-start | bytes 13828
  2.4 6.0 %copy-start.4 = (bf16[17,16]{0,1:T(8,128)(2,1)S(1)}, bf16[17,16]{0,1:T(8,128)(2,1)}, u32[]{:S(2)}) copy-start(bf16[17,16]{0,1:T(8,128)(2,1)} %param.13) | copy-start | bytes 1636
  2.4 7.4 %collective-permute-start.3 = (bf16[528,256]{1,0:T(8,128)(2,1)}, bf16[528,256]{1,0:T(8,128)(2,1)S(1)}, u32[]{:S(2)}, u32[]{:S(2)}) collective-permute-start(bf16[528,256]{1,0:T(8,128)(2,1)} %shard_map.74.own0), channel_id=1, source_target_pairs={{0,1},{1,0},{2,3},{3,2},{4,5},{5,4},{6,7},{7,6},{8,9},{9,8},{10,11... | collective-permute-start | bytes 811016 | tf_op jit(solution)/shard_map/ppermute | solution.py:287
  2.9 10.1 %collective-permute-start.2 = (bf16[528,256]{1,0:T(8,128)(2,1)}, bf16[528,256]{1,0:T(8,128)(2,1)S(1)}, u32[]{:S(2)}, u32[]{:S(2)}) collective-permute-start(bf16[528,256]{1,0:T(8,128)(2,1)} %shard_map.74.own0), channel_id=1, source_target_pairs={{0,2},{2,0},{4,6},{6,4},{8,10},{10,8},{12,14},{14,12},{1,3},{3,1},... | collective-permute-start | bytes 811016 | tf_op jit(solution)/shard_map/ppermute | solution.py:289
  7.9 1.9 %collective-permute-start.4 = (bf16[528,256]{1,0:T(8,128)(2,1)}, bf16[528,256]{1,0:T(8,128)(2,1)S(1)}, u32[]{:S(2)}, u32[]{:S(2)}) collective-permute-start(bf16[528,256]{1,0:T(8,128)(2,1)} %shard_map.73.own1), channel_id=1, source_target_pairs={{0,1},{1,0},{2,3},{3,2},{4,5},{5,4},{6,7},{7,6},{8,9},{9,8},{10,11... | collective-permute-start | bytes 811016 | tf_op jit(solution)/shard_map/ppermute | solution.py:287
  8.1 10.5 %collective-permute-start = (bf16[528,256]{1,0:T(8,128)(2,1)}, bf16[528,256]{1,0:T(8,128)(2,1)S(1)}, u32[]{:S(2)}, u32[]{:S(2)}) collective-permute-start(bf16[528,256]{1,0:T(8,128)(2,1)} %shard_map.73.own1), channel_id=1, source_target_pairs={{0,2},{2,0},{4,6},{6,4},{8,10},{10,8},{12,14},{14,12},{1,3},{3,1},... | collective-permute-start | bytes 811016 | tf_op jit(solution)/shard_map/ppermute | solution.py:289
  8.4 1.4 %copy-start = (bf16[528,256]{1,0:T(8,128)(2,1)S(1)}, bf16[528,256]{1,0:T(8,128)(2,1)}, u32[]{:S(2)}) copy-start(bf16[528,256]{1,0:T(8,128)(2,1)} %shard_map.74.own0) | copy-start | bytes 811012
  8.4 1.5 %copy-start.1 = (bf16[528,256]{1,0:T(8,128)(2,1)S(1)}, bf16[528,256]{1,0:T(8,128)(2,1)}, u32[]{:S(2)}) copy-start(bf16[528,256]{1,0:T(8,128)(2,1)} %shard_map.73.own1) | copy-start | bytes 811012
  13.1 9.8 %collective-permute-start.7 = (bf16[528,256]{1,0:T(8,128)(2,1)S(1)}, bf16[528,256]{1,0:T(8,128)(2,1)S(1)}, u32[]{:S(2)}, u32[]{:S(2)}) collective-permute-start(bf16[528,256]{1,0:T(8,128)(2,1)S(1)} %collective-permute-done.2.par0), channel_id=1, source_target_pairs={{0,4},{4,8},{6,2},{8,12},{10,6},{14,10},{1,5},{5,9},{7,3},{9,13},{... | collective-permute-start | bytes 811016 | tf_op jit(solution)/shard_map/ppermute | solution.py:328
  18.6 4.3 %collective-permute-start.6 = (bf16[528,256]{1,0:T(8,128)(2,1)S(1)}, bf16[528,256]{1,0:T(8,128)(2,1)S(1)}, u32[]{:S(2)}, u32[]{:S(2)}) collective-permute-start(bf16[528,256]{1,0:T(8,128)(2,1)S(1)} %collective-permute-done.par1), channel_id=1, source_target_pairs={{0,1},{1,0},{2,3},{3,2},{4,5},{5,4},{6,7},{7,6},{8,9},{9,8},{10,11... | collective-permute-start | bytes 811016 | tf_op jit(solution)/shard_map/ppermute | solution.py:287
  18.6 4.3 %collective-permute-start.5 = (bf16[528,256]{1,0:T(8,128)(2,1)S(1)}, bf16[528,256]{1,0:T(8,128)(2,1)S(1)}, u32[]{:S(2)}, u32[]{:S(2)}) collective-permute-start(bf16[528,256]{1,0:T(8,128)(2,1)S(1)} %collective-permute-done.2.par0), channel_id=1, source_target_pairs={{0,1},{1,0},{2,3},{3,2},{4,5},{5,4},{6,7},{7,6},{8,9},{9,8},{10,11... | collective-permute-start | bytes 811016 | tf_op jit(solution)/shard_map/ppermute | solution.py:287
  19.1 9.6 %collective-permute-start.1 = (bf16[528,256]{1,0:T(8,128)(2,1)S(1)}, bf16[528,256]{1,0:T(8,128)(2,1)S(1)}, u32[]{:S(2)}, u32[]{:S(2)}) collective-permute-start(bf16[528,256]{1,0:T(8,128)(2,1)S(1)} %collective-permute-done.par1), channel_id=1, source_target_pairs={{0,4},{4,8},{6,2},{8,12},{10,6},{14,10},{1,5},{5,9},{7,3},{9,13},{... | collective-permute-start | bytes 811016 | tf_op jit(solution)/shard_map/ppermute | solution.py:328
  22.9 6.1 %collective-permute-start.9 = (bf16[528,256]{1,0:T(8,128)(2,1)S(1)}, bf16[528,256]{1,0:T(8,128)(2,1)S(1)}, u32[]{:S(2)}, u32[]{:S(2)}) collective-permute-start(bf16[528,256]{1,0:T(8,128)(2,1)S(1)} %collective-permute-done.7.xs), channel_id=1, source_target_pairs={{0,1},{1,0},{2,3},{3,2},{4,5},{5,4},{6,7},{7,6},{8,9},{9,8},{10,11... | collective-permute-start | bytes 811016 | tf_op jit(solution)/shard_map/ppermute | solution.py:287
  28.7 1.6 %collective-permute-start.8 = (bf16[528,256]{1,0:T(8,128)(2,1)S(1)}, bf16[528,256]{1,0:T(8,128)(2,1)S(1)}, u32[]{:S(2)}, u32[]{:S(2)}) collective-permute-start(bf16[528,256]{1,0:T(8,128)(2,1)S(1)} %collective-permute-done.1.far1), channel_id=1, source_target_pairs={{0,1},{1,0},{2,3},{3,2},{4,5},{5,4},{6,7},{7,6},{8,9},{9,8},{10,11... | collective-permute-start | bytes 811016 | tf_op jit(solution)/shard_map/ppermute | solution.py:287

commit v6 on v5

--- a/solution.py
+++ b/solution.py
@@ -87,13 +87,13 @@
             a = spread(xs[x0 : x0 + 16, :])
             hi = lax.dot_general(a, xs[right, :], NT, preferred_element_type=F32)
             lo = lax.dot_general(a, left_zero[...], NT, preferred_element_type=F32)
-            m = masks[k : k + 1]
+            m = masks[k : k + 1].astype(BF)
             for i in range(16):
                 x = x0 + i
                 s = jnp.where(lane <= x, hi[i * G : i * G + G], lo[i * G : i * G + G])
                 if x < ndisp - 1:
                     s = pltpu.roll(s, ndisp - 1 - x, 1)
-                put(x + 2, s * m)
+                put(x + 2, s.astype(BF) * m)
 
         mask_n = xn[2 * cols : 2 * cols + 16, :].astype(F32)
         tail = xn[cols - 16 : cols, :].astype(F32)[14:16]

time: 39.3 us -> 39.3 us (level)
  no operation moved by 1% of the time
where the time goes in v6:
time: 39.3 us; the launch traced here: 39 us
  Pallas kernels  24.2 us (62%)
  starting transfers between devices  12.2 us (31%)
  waiting for transfers between devices  2.44 us (6%)
    pallas_call x1, Pallas kernels, body(): pl.pallas_call(last_kernel, out_shape=jax.ShapeDtypeStruct((row_count, co...  8.57 us
    ppermute x2, starting transfers between devices, send_on(): return lax.ppermute(x, 'rows', onward)  7.64 us
    pallas_call x1, Pallas kernels, body(): pl.pallas_call(partner_kernel, out_shape=jax.ShapeDtypeStruct(pair, BF),...  5.54 us
    pallas_call x2, Pallas kernels, body(): pl.pallas_call(functools.partial(pack_kernel, c), out_shape=packed, in_sp...  4.74 us
    ppermute x2, starting transfers between devices, body(): par0, par1 = [lax.ppermute(x, 'rows', partners) for x in chunks]  2.86 us
    pallas_call x1, Pallas kernels, body(): pl.pallas_call(own_kernel, out_shape=[volume_out] * 2, in_specs=[VMEM] *...  2.59 us
    ppermute x2, waiting for transfers between devices, body(): par0, par1 = [lax.ppermute(x, 'rows', partners) for x in chunks]  2.2 us
    ppermute x6, starting transfers between devices, cross(): return lax.ppermute(x, 'cols', across)  1.68 us
  transfers between devices with their start and end apart: 10, of which 3 were waited for; matrix products, arithmetic and copies ran while one was open for 0% of the time, Pallas kernels for 34%

profile of v6, /device:TPU:0, one launch (start us, length us, event | category | flops | bytes accessed | tf_op | source)
XLA Modules:
  0.0 39.0 jit_solution(16426149126903119236)
XLA Ops:
  0.0 2.4 %shard_map.74.own0 = bf16[528,256]{1,0:T(8,128)(2,1)} custom-call(bf16[2,256,256]{2,1,0:T(8,128)(2,1)} %left.3, bf16[2,256,256]{2,1,0:T(8,128)(2,1)} %right.3, s32[1,2,4]{2,1,0:T(2,128)} %bitcast.3, s32[1,4]{1,0:T(1,128)} %block_count.3), custom_call_target="tpu_custom_call" | custom-call | flops 1000000000 | bytes 1000000 | tf_op jit(solution)/shard_map/pallas_call | solution.py:270
  2.4 0.0 copy-start.2
  2.4 0.0 copy-start.3
  2.4 0.0 copy-start.4
  2.4 0.5 %collective-permute-start.3 = (bf16[528,256]{1,0:T(8,128)(2,1)}, bf16[528,256]{1,0:T(8,128)(2,1)S(1)}, u32[]{:S(2)}, u32[]{:S(2)}) collective-permute-start(bf16[528,256]{1,0:T(8,128)(2,1)} %shard_map.74.own0), channel_id=1, source_target_pairs={{0,1},{1,0},{2,3},{3,2},{4,5},{5,4},{6,7},{7,6},{8,9},{9,8},{10,11... | collective-permute-start | bytes 811016 | tf_op jit(solution)/shard_map/ppermute | solution.py:287
  2.9 2.6 %collective-permute-start.2 = (bf16[528,256]{1,0:T(8,128)(2,1)}, bf16[528,256]{1,0:T(8,128)(2,1)S(1)}, u32[]{:S(2)}, u32[]{:S(2)}) collective-permute-start(bf16[528,256]{1,0:T(8,128)(2,1)} %shard_map.74.own0), channel_id=1, source_target_pairs={{0,2},{2,0},{4,6},{6,4},{8,10},{10,8},{12,14},{14,12},{1,3},{3,1},... | collective-permute-start | bytes 811016 | tf_op jit(solution)/shard_map/ppermute | solution.py:289
  5.5 2.4 %shard_map.73.own1 = bf16[528,256]{1,0:T(8,128)(2,1)} custom-call(bf16[2,256,256]{2,1,0:T(8,128)(2,1)} %left.3, bf16[2,256,256]{2,1,0:T(8,128)(2,1)} %right.3, s32[1,2,4]{2,1,0:T(2,128)} %bitcast.4, s32[1,4]{1,0:T(1,128)} %block_count.3), custom_call_target="tpu_custom_call" | custom-call | flops 1000000000 | bytes 1000000 | tf_op jit(solution)/shard_map/pallas_call | solution.py:270
  7.9 0.2 collective-permute-start.4
  8.1 0.3 collective-permute-start
  8.4 0.0 copy-done.2
  8.4 0.0 copy-done.3
  8.4 0.0 copy-done.4
  8.4 0.0 copy-start
  8.4 0.0 copy-start.1
  8.4 1.4 %shard_map.75 = (bf16[2,192,256]{2,1,0:T(8,128)(2,1)S(1)}, bf16[3,128,480]{2,1,0:T(8,128)(2,1)S(1)}, bf16[4096,256]{1,0:T(8,128)(2,1)S(1)}) custom-call(bf16[3,3,16,16]{3,2,1,0:T(8,128)(2,1)S(1)} %copy-done.2, bf16[3,3,16,16]{3,2,1,0:T(8,128)(2,1)S(1)} %copy-done.3, bf16[16,17]{1,0:T(8,128)(2,1)S(1)} %bitcast.2), custom_call_target="tpu_custom_call" | custom-call | flops 4000000000 | bytes 4000000 | tf_op jit(solution)/shard_map/pallas_call | solution.py:299
  9.8 0.0 collective-permute-done.3.own0_n
  9.8 0.0 collective-permute-done.4.own1_n
  9.9 0.0 copy-done
  9.9 0.0 copy-done.1
  9.9 2.6 %shard_map.76 = (bf16[260,16,256]{2,1,0:T(8,128)(2,1)S(1)}, bf16[260,16,256]{2,1,0:T(8,128)(2,1)S(1)}) custom-call(bf16[528,256]{1,0:T(8,128)(2,1)S(1)} %copy-done, bf16[528,256]{1,0:T(8,128)(2,1)S(1)} %copy-done.1, bf16[528,256]{1,0:T(8,128)(2,1)S(1)} %collective-permute-done.3.own0_n, bf16[528,256]{1,0:T(8,128)(2,1)S(1)} %collective-permute-done.4.own1_n), custom_call_target="tpu_custom_call" | custom-call | flops 4000000000 | bytes 4000000 | tf_op jit(solution)/shard_map/pallas_call | solution.py:312
  12.5 0.6 %collective-permute-done.2.par0 = bf16[528,256]{1,0:T(8,128)(2,1)S(1)} collective-permute-done((bf16[528,256]{1,0:T(8,128)(2,1)}, bf16[528,256]{1,0:T(8,128)(2,1)S(1)}, u32[]{:S(2)}, u32[]{:S(2)}) %collective-permute-start.2) | collective-permute-done | bytes 270368 | tf_op jit(solution)/shard_map/ppermute | solution.py:289
  13.1 3.9 %collective-permute-start.7 = (bf16[528,256]{1,0:T(8,128)(2,1)S(1)}, bf16[528,256]{1,0:T(8,128)(2,1)S(1)}, u32[]{:S(2)}, u32[]{:S(2)}) collective-permute-start(bf16[528,256]{1,0:T(8,128)(2,1)S(1)} %collective-permute-done.2.par0), channel_id=1, source_target_pairs={{0,4},{4,8},{6,2},{8,12},{10,6},{14,10},{1,5},{5,9},{7,3},{9,13},{... | collective-permute-start | bytes 811016 | tf_op jit(solution)/shard_map/ppermute | solution.py:328
  17.0 1.6 %collective-permute-done.par1 = bf16[528,256]{1,0:T(8,128)(2,1)S(1)} collective-permute-done((bf16[528,256]{1,0:T(8,128)(2,1)}, bf16[528,256]{1,0:T(8,128)(2,1)S(1)}, u32[]{:S(2)}, u32[]{:S(2)}) %collective-permute-start) | collective-permute-done | bytes 270368 | tf_op jit(solution)/shard_map/ppermute | solution.py:289
  18.6 0.0 collective-permute-start.6
  18.6 0.5 %collective-permute-start.5 = (bf16[528,256]{1,0:T(8,128)(2,1)S(1)}, bf16[528,256]{1,0:T(8,128)(2,1)S(1)}, u32[]{:S(2)}, u32[]{:S(2)}) collective-permute-start(bf16[528,256]{1,0:T(8,128)(2,1)S(1)} %collective-permute-done.2.par0), channel_id=1, source_target_pairs={{0,1},{1,0},{2,3},{3,2},{4,5},{5,4},{6,7},{7,6},{8,9},{9,8},{10,11... | collective-permute-start | bytes 811016 | tf_op jit(solution)/shard_map/ppermute | solution.py:287
  19.1 3.7 %collective-permute-start.1 = (bf16[528,256]{1,0:T(8,128)(2,1)S(1)}, bf16[528,256]{1,0:T(8,128)(2,1)S(1)}, u32[]{:S(2)}, u32[]{:S(2)}) collective-permute-start(bf16[528,256]{1,0:T(8,128)(2,1)S(1)} %collective-permute-done.par1), channel_id=1, source_target_pairs={{0,4},{4,8},{6,2},{8,12},{10,6},{14,10},{1,5},{5,9},{7,3},{9,13},{... | collective-permute-start | bytes 811016 | tf_op jit(solution)/shard_map/ppermute | solution.py:328
  22.8 0.0 collective-permute-done.7.xs
  22.9 0.0 collective-permute-done.6.par1_n
  22.9 0.1 collective-permute-start.9
  22.9 0.0 collective-permute-done.5.par0_n
  23.0 5.5 %shard_map.77.partner = bf16[258,32,256]{2,1,0:T(8,128)(2,1)S(1)} custom-call(bf16[528,256]{1,0:T(8,128)(2,1)S(1)} %collective-permute-done.2.par0, bf16[528,256]{1,0:T(8,128)(2,1)S(1)} %collective-permute-done.par1, bf16[528,256]{1,0:T(8,128)(2,1)S(1)} %collective-permute-done.5.par0_n, bf16[528,256]{1,0:T(8,128)(2,1)S(1)} %collective-permute-done.6.par1_n, ...), custom_call_target="tpu_custom_call" | custom-call | flops 8000000000 | bytes 8000000 | tf_op jit(solution)/shard_map/pallas_call | solution.py:337
  28.5 0.2 collective-permute-done.1.far1
  28.7 0.4 collective-permute-start.8
  29.1 0.0 collective-permute-done.9.xn
  29.1 1.4 %shard_map.78.f0 = bf16[260,16,256]{2,1,0:T(8,128)(2,1)S(1)} custom-call(bf16[528,256]{1,0:T(8,128)(2,1)S(1)} %collective-permute-done.7.xs, bf16[528,256]{1,0:T(8,128)(2,1)S(1)} %collective-permute-done.9.xn), custom_call_target="tpu_custom_call" | custom-call | flops 1000000000 | bytes 1000000 | tf_op jit(solution)/shard_map/pallas_call | solution.py:348
  30.5 0.0 collective-permute-done.8.far1_n
  30.5 8.6 %shard_map.79 = f32[2,256,256]{2,1,0:T(8,128)} custom-call(bf16[528,256]{1,0:T(8,128)(2,1)S(1)} %collective-permute-done.1.far1, bf16[528,256]{1,0:T(8,128)(2,1)S(1)} %collective-permute-done.8.far1_n, bf16[260,16,256]{2,1,0:T(8,128)(2,1)S(1)} %shard_map.78.f0, bf16[260,16,256]{2,1,0:T(8,128)(2,1)S(1)} %get-tuple-element.21.o0, ...), custom_call_target="tpu_custom_call" | custom-call | flops 12000000000 | bytes 12000000 | tf_op jit(solution)/shard_map/pallas_call | solution.py:358
Async XLA Ops:
  2.4 6.0 %copy-start.2 = (bf16[3,3,16,16]{3,2,1,0:T(8,128)(2,1)S(1)}, bf16[3,3,16,16]{3,2,1,0:T(8,128)(2,1)}, u32[]{:S(2)}) copy-start(bf16[3,3,16,16]{3,2,1,0:T(8,128)(2,1)} %s1_.1) | copy-start | bytes 13828
  2.4 6.0 %copy-start.3 = (bf16[3,3,16,16]{3,2,1,0:T(8,128)(2,1)S(1)}, bf16[3,3,16,16]{3,2,1,0:T(8,128)(2,1)}, u32[]{:S(2)}) copy-start(bf16[3,3,16,16]{3,2,1,0:T(8,128)(2,1)} %s2_.1) | copy-start | bytes 13828
  2.4 6.0 %copy-start.4 = (bf16[17,16]{0,1:T(8,128)(2,1)S(1)}, bf16[17,16]{0,1:T(8,128)(2,1)}, u32[]{:S(2)}) copy-start(bf16[17,16]{0,1:T(8,128)(2,1)} %param.13) | copy-start | bytes 1636
  2.4 7.4 %collective-permute-start.3 = (bf16[528,256]{1,0:T(8,128)(2,1)}, bf16[528,256]{1,0:T(8,128)(2,1)S(1)}, u32[]{:S(2)}, u32[]{:S(2)}) collective-permute-start(bf16[528,256]{1,0:T(8,128)(2,1)} %shard_map.74.own0), channel_id=1, source_target_pairs={{0,1},{1,0},{2,3},{3,2},{4,5},{5,4},{6,7},{7,6},{8,9},{9,8},{10,11... | collective-permute-start | bytes 811016 | tf_op jit(solution)/shard_map/ppermute | solution.py:287
  2.9 10.1 %collective-permute-start.2 = (bf16[528,256]{1,0:T(8,128)(2,1)}, bf16[528,256]{1,0:T(8,128)(2,1)S(1)}, u32[]{:S(2)}, u32[]{:S(2)}) collective-permute-start(bf16[528,256]{1,0:T(8,128)(2,1)} %shard_map.74.own0), channel_id=1, source_target_pairs={{0,2},{2,0},{4,6},{6,4},{8,10},{10,8},{12,14},{14,12},{1,3},{3,1},... | collective-permute-start | bytes 811016 | tf_op jit(solution)/shard_map/ppermute | solution.py:289
  7.9 1.9 %collective-permute-start.4 = (bf16[528,256]{1,0:T(8,128)(2,1)}, bf16[528,256]{1,0:T(8,128)(2,1)S(1)}, u32[]{:S(2)}, u32[]{:S(2)}) collective-permute-start(bf16[528,256]{1,0:T(8,128)(2,1)} %shard_map.73.own1), channel_id=1, source_target_pairs={{0,1},{1,0},{2,3},{3,2},{4,5},{5,4},{6,7},{7,6},{8,9},{9,8},{10,11... | collective-permute-start | bytes 811016 | tf_op jit(solution)/shard_map/ppermute | solution.py:287
  8.1 10.5 %collective-permute-start = (bf16[528,256]{1,0:T(8,128)(2,1)}, bf16[528,256]{1,0:T(8,128)(2,1)S(1)}, u32[]{:S(2)}, u32[]{:S(2)}) collective-permute-start(bf16[528,256]{1,0:T(8,128)(2,1)} %shard_map.73.own1), channel_id=1, source_target_pairs={{0,2},{2,0},{4,6},{6,4},{8,10},{10,8},{12,14},{14,12},{1,3},{3,1},... | collective-permute-start | bytes 811016 | tf_op jit(solution)/shard_map/ppermute | solution.py:289
  8.4 1.4 %copy-start = (bf16[528,256]{1,0:T(8,128)(2,1)S(1)}, bf16[528,256]{1,0:T(8,128)(2,1)}, u32[]{:S(2)}) copy-start(bf16[528,256]{1,0:T(8,128)(2,1)} %shard_map.74.own0) | copy-start | bytes 811012
  8.4 1.5 %copy-start.1 = (bf16[528,256]{1,0:T(8,128)(2,1)S(1)}, bf16[528,256]{1,0:T(8,128)(2,1)}, u32[]{:S(2)}) copy-start(bf16[528,256]{1,0:T(8,128)(2,1)} %shard_map.73.own1) | copy-start | bytes 811012
  13.1 9.8 %collective-permute-start.7 = (bf16[528,256]{1,0:T(8,128)(2,1)S(1)}, bf16[528,256]{1,0:T(8,128)(2,1)S(1)}, u32[]{:S(2)}, u32[]{:S(2)}) collective-permute-start(bf16[528,256]{1,0:T(8,128)(2,1)S(1)} %collective-permute-done.2.par0), channel_id=1, source_target_pairs={{0,4},{4,8},{6,2},{8,12},{10,6},{14,10},{1,5},{5,9},{7,3},{9,13},{... | collective-permute-start | bytes 811016 | tf_op jit(solution)/shard_map/ppermute | solution.py:328
  18.6 4.3 %collective-permute-start.6 = (bf16[528,256]{1,0:T(8,128)(2,1)S(1)}, bf16[528,256]{1,0:T(8,128)(2,1)S(1)}, u32[]{:S(2)}, u32[]{:S(2)}) collective-permute-start(bf16[528,256]{1,0:T(8,128)(2,1)S(1)} %collective-permute-done.par1), channel_id=1, source_target_pairs={{0,1},{1,0},{2,3},{3,2},{4,5},{5,4},{6,7},{7,6},{8,9},{9,8},{10,11... | collective-permute-start | bytes 811016 | tf_op jit(solution)/shard_map/ppermute | solution.py:287
  18.6 4.3 %collective-permute-start.5 = (bf16[528,256]{1,0:T(8,128)(2,1)S(1)}, bf16[528,256]{1,0:T(8,128)(2,1)S(1)}, u32[]{:S(2)}, u32[]{:S(2)}) collective-permute-start(bf16[528,256]{1,0:T(8,128)(2,1)S(1)} %collective-permute-done.2.par0), channel_id=1, source_target_pairs={{0,1},{1,0},{2,3},{3,2},{4,5},{5,4},{6,7},{7,6},{8,9},{9,8},{10,11... | collective-permute-start | bytes 811016 | tf_op jit(solution)/shard_map/ppermute | solution.py:287
  19.1 9.6 %collective-permute-start.1 = (bf16[528,256]{1,0:T(8,128)(2,1)S(1)}, bf16[528,256]{1,0:T(8,128)(2,1)S(1)}, u32[]{:S(2)}, u32[]{:S(2)}) collective-permute-start(bf16[528,256]{1,0:T(8,128)(2,1)S(1)} %collective-permute-done.par1), channel_id=1, source_target_pairs={{0,4},{4,8},{6,2},{8,12},{10,6},{14,10},{1,5},{5,9},{7,3},{9,13},{... | collective-permute-start | bytes 811016 | tf_op jit(solution)/shard_map/ppermute | solution.py:328
  22.9 6.2 %collective-permute-start.9 = (bf16[528,256]{1,0:T(8,128)(2,1)S(1)}, bf16[528,256]{1,0:T(8,128)(2,1)S(1)}, u32[]{:S(2)}, u32[]{:S(2)}) collective-permute-start(bf16[528,256]{1,0:T(8,128)(2,1)S(1)} %collective-permute-done.7.xs), channel_id=1, source_target_pairs={{0,1},{1,0},{2,3},{3,2},{4,5},{5,4},{6,7},{7,6},{8,9},{9,8},{10,11... | collective-permute-start | bytes 811016 | tf_op jit(solution)/shard_map/ppermute | solution.py:287
  28.7 1.7 %collective-permute-start.8 = (bf16[528,256]{1,0:T(8,128)(2,1)S(1)}, bf16[528,256]{1,0:T(8,128)(2,1)S(1)}, u32[]{:S(2)}, u32[]{:S(2)}) collective-permute-start(bf16[528,256]{1,0:T(8,128)(2,1)S(1)} %collective-permute-done.1.far1), channel_id=1, source_target_pairs={{0,1},{1,0},{2,3},{3,2},{4,5},{5,4},{6,7},{7,6},{8,9},{9,8},{10,11... | collective-permute-start | bytes 811016 | tf_op jit(solution)/shard_map/ppermute | solution.py:287
